TPU v7x, 128 devices: a whole 4x4x4 slice. The times are simulated.
128 devices in a mesh: dp: 16 (over z, y), rep: 8 (over x, core).
Axes of the slice: x: 4, y: 4, z: 4, core: 2. Of those that a mesh axis runs over, the one named last changes fastest.
Arguments:
- hidden: bfloat16 [49152, 4096], P(('dp', 'rep')), may hold values from -6 to 6
- step_slot: int32 [49152], P(('dp', 'rep')), may hold values from 0 to 79, as said below
- positive: int32 [10240], P(('dp', 'rep')), may hold values from 0 to 10239, as said below
- proj: bfloat16 [4096, 1024], replicated, may hold values from -0.09375 to 0.09375
Outputs:
- hidden_grad: bfloat16 [49152, 4096], P(('dp', 'rep'))
- proj_grad: float32 [4096, 1024], P(('dp', 'rep'))
- loss: float32 [], replicated
Inputs may be any that keep to these rules, and one draw needn't show every extreme that they name: `step_slot`: each solution owns 40 consecutive slots of its device and fills its first k of them, 2 <= k <= 40, with runs of consecutive tokens in order; some device has all its solutions at 40 steps. `positive`: for a live slot, another live slot of the same solution; for a slot that is not live, its own index.
All inputs are finite; a program needn't handle non-finite values.
Results may differ from a plain program's by a relative error of at most 0.0086.
Values may be sent and summed in bfloat16 or wider, within the bound.
A program may use at most 128 MiB of HBM per device.

v0:
```python
import math

import jax
import jax.numpy as jnp
from jax import lax
from jax.sharding import PartitionSpec as P

sharpness_divisor = 0.3


def local(hidden, step_slot, positive, proj):
    cap = positive.shape[0]
    tok_rows = hidden.shape[0]
    feature_size = proj.shape[1]
    similarity_multiplier = 1.0 / (sharpness_divisor * math.sqrt(feature_size))
    member = step_slot[None, :] == lax.broadcasted_iota(jnp.int32, (cap, tok_rows), 0)
    onehot = member.astype(jnp.bfloat16)
    step_counts = jnp.sum(member.astype(jnp.int32), axis=1)
    denom = jnp.maximum(step_counts, 1).astype(jnp.float32)
    pooled = (jnp.dot(onehot, hidden, preferred_element_type=jnp.float32) / denom[:, None]).astype(
        jnp.bfloat16
    )
    embed = jnp.dot(pooled, proj, preferred_element_type=jnp.float32)
    reciprocal_scale = lax.rsqrt(jnp.mean(embed * embed, axis=1) + 1e-06)
    unit = embed * reciprocal_scale[:, None]
    unit_b = unit.astype(jnp.bfloat16)
    own_ids = lax.axis_index(("dp", "rep")) * cap + jnp.arange(cap, dtype=jnp.int32)
    live = step_counts > 0
    all_unit, overall_tallies, all_pos = (
        lax.all_gather(unit_b, ("dp", "rep"), axis=0, tiled=True),
        lax.all_gather(step_counts, ("dp", "rep"), axis=0, tiled=True),
        lax.all_gather(positive, ("dp", "rep"), axis=0, tiled=True),
    )
    scores = (
        lax.dot_general(
            unit_b, all_unit, (((1,), (1,)), ((), ())), preferred_element_type=jnp.float32
        )
        * similarity_multiplier
    )
    col_ids = jnp.arange(all_unit.shape[0], dtype=jnp.int32)
    mask = (overall_tallies > 0)[None, :] & (col_ids[None, :] != own_ids[:, None])
    scores, mask, col_ids = (scores, mask, col_ids)
    lse = jnp.log(jnp.sum(jnp.where(mask, jnp.exp(scores), 0.0), axis=1))
    onepos = (col_ids[None, :] == positive[:, None]).astype(jnp.float32)
    picked = jnp.sum(scores * onepos, axis=1)
    nlive = jnp.sum((overall_tallies > 0).astype(jnp.float32))
    global_normalizer_value = lax.all_gather(lse, ("dp", "rep"), axis=0, tiled=True)
    onepos = (col_ids[None, :] == positive[:, None]).astype(jnp.float32)
    rowpart = jnp.where(
        live[:, None], jnp.where(mask, jnp.exp(scores - lse[:, None]), 0.0) - onepos, 0.0
    )
    colmask = live[:, None] & (col_ids[None, :] != own_ids[:, None])
    backpos = (all_pos[None, :] == own_ids[:, None]).astype(jnp.float32)
    colpart = jnp.where(
        (overall_tallies > 0)[None, :],
        jnp.where(colmask, jnp.exp(scores - global_normalizer_value[None, :]), 0.0) - backpos,
        0.0,
    )
    weights = ((rowpart + colpart) / nlive).astype(jnp.bfloat16)
    unit_grad = (
        jnp.dot(weights, all_unit, preferred_element_type=jnp.float32) * similarity_multiplier
    )
    loss = lax.psum(jnp.sum(jnp.where(live, lse - picked, 0.0)), ("dp", "rep")) / nlive
    inner = jnp.mean(unit * unit_grad, axis=1, keepdims=True)
    embed_grad = (reciprocal_scale[:, None] * (unit_grad - unit * inner)).astype(jnp.bfloat16)
    proj_grad = lax.psum_scatter(
        lax.dot_general(
            pooled, embed_grad, (((0,), (0,)), ((), ())), preferred_element_type=jnp.float32
        ),
        ("dp", "rep"),
        scatter_dimension=0,
        tiled=True,
    )
    pooled_grad = lax.dot_general(
        embed_grad, proj, (((1,), (1,)), ((), ())), preferred_element_type=jnp.float32
    )
    pooled_grad = (pooled_grad / denom[:, None]).astype(jnp.bfloat16)
    hidden_grad = lax.dot_general(
        onehot, pooled_grad, (((0,), (0,)), ((), ())), preferred_element_type=jnp.float32
    )
    return (hidden_grad.astype(jnp.bfloat16), proj_grad, loss)


def solution(mesh):
    in_specs = (P(("dp", "rep"), None), P(("dp", "rep")), P(("dp", "rep")), P())
    out_specs = (P(("dp", "rep"), None), P(("dp", "rep"), None), P())
    return jax.shard_map(local, mesh=mesh, in_specs=in_specs, out_specs=out_specs, check_vma=False)
```

profile of v0, /device:TPU:0, one launch (start us, length us, event | category | flops | bytes accessed | tf_op | source)
XLA Modules:
  0.0 1015.9 jit_solution(12543600453659764995)
XLA Ops:
  7.2 0.0 copy-start
  7.2 0.0 all-reduce.7.cloned.1.call-start
  7.2 0.9 convert_reduce_fusion
  8.2 0.0 copy-start.8
  8.2 0.3 dynamic-update-slice
  8.5 0.0 copy-start.6
  8.5 0.9 dynamic-update-slice.2
  9.4 0.0 copy-start.5
  9.4 0.0 copy-done.6
  9.4 0.6 copy-done.5
  10.0 0.0 all-reduce.7.cloned.1.call-update
  10.0 0.0 all-gather.2.cloned.1.call-start
  10.1 0.0 copy-done.8
  10.1 0.0 copy-done
  10.1 1.4 fusion
  11.5 0.0 copy-start.1
  11.5 0.0 copy-start.9
  11.5 0.0 copy-start.10
  11.5 5.3 multiply_reduce_fusion.1
  16.8 0.0 copy-done.1
  16.9 0.7 multiply_convert_fusion.1
  17.6 0.0 all-gather.2.cloned.1.call-update
  17.6 0.0 reduce-scatter.2.cloned.1.call-start
  17.7 0.0 copy-done.9
  17.7 135.7 %all-reduce.7.cloned.1.call-done = (s32[10240]{0:T(1024)}, s32[10240]{0:T(1024)}) async-done(((s32[10240]{0:T(1024)}, s32[10240]{0:T(1024)}), (s32[10240]{0:T(1024)}, s32[10240]{0:T(1024)})) %all-reduce.7.cloned.1.call-update) | async-done | bytes 81936
  153.4 1.4 convert_reduce_fusion.1
  154.8 87.7 %all-gather.2.cloned.1.call-done = bf16[10240,1024]{1,0:T(8,128)(2,1)} async-done(((bf16[80,1024]{1,0:T(8,128)(2,1)}), bf16[10240,1024]{1,0:T(8,128)(2,1)}) %all-gather.2.cloned.1.call-update) | async-done | bytes 20971536 | tf_op jit(solution)/shard_map/all_gather | solution.py:30
  242.4 0.0 copy-done.10
  242.4 12.4 %select_reduce_fusion = (f32[80]{0:T(128)S(1)}, f32[80]{0:T(128)S(1)}, f32[80,10240]{1,0:T(8,128)}) fusion(s32[80]{0:T(128)S(1)} %copy-done.10, s32[80]{0:T(128)S(1)} %iota_add_fusion, pred[10240]{0:T(1024)(128)(4,1)S(1)} %get-tuple-element.10, bf16[80,1024]{1,0:T(8,128)(2,1)} %multiply_convert_fusion.1, bf16[10240,1024]{1,0:T(8,128)(2,1)} %all-gather.2.cloned.1.call-done), kind=kOutput, calls=%fused_computation.6 | convolution fusion | flops 1684274944 | bytes 24423680 | tf_op jit(solution)/shard_map/dot_general | solution.py:35
  254.8 0.8 fusion.19
  255.6 65.5 %all-reduce.4 = (f32[10240]{0:T(1024)}, f32[]{:T(128)}) all-reduce(f32[10240]{0:T(1024)S(1)} %get-tuple-element.12, f32[]{:T(128)} %get-tuple-element.13), channel_id=1, replica_groups=mesh['dp'=16,'rep'=8] {'dp','rep'}, use_global_device_ids=true, to_apply=%add.1 | all-reduce | flops 10241 | bytes 81928
  321.1 0.0 copy-start.2
  321.1 14.1 %multiply_reduce_fusion = (f32[80]{0:T(128)S(1)}, f32[80,1024]{1,0:T(8,128)S(1)}) fusion(f32[80,1024]{1,0:T(8,128)S(1)} %get-tuple-element.15, f32[80]{0:T(128)S(1)} %add_rsqrt_fusion, bf16[10240,1024]{1,0:T(8,128)(2,1)} %all-gather.2.cloned.1.call-done, f32[80,10240]{1,0:T(8,128)} %get-tuple-element.16, f32[]{:T(128)} %get-tuple-element.9, ...), kind=kOutput, calls=%fused_computation.26 | convolution fusion | flops 1692794752 | bytes 24997524 | tf_op jit(solution)/shard_map/dot_general | solution.py:61
  335.2 0.1 multiply_convert_fusion
  335.4 0.0 copy-start.3
  335.4 0.6 copy-done.3
  336.0 0.0 copy-done.2
  336.0 8.1 fusion.20
  344.1 0.0 copy-start.4
  344.1 0.0 copy-start.7
  344.1 0.0 reduce-scatter.2.cloned.1.call-update
  345.6 0.0 copy-done.4
  345.6 0.0 copy-done.7
  345.6 8.5 convolution_convert_fusion
  354.1 654.1 %reduce-scatter.2.cloned.1.call-done = f32[32,1024]{1,0:T(8,128)} async-done(((f32[4096,1024]{1,0:T(8,128)}), f32[32,1024]{1,0:T(8,128)}) %reduce-scatter.2.cloned.1.call-update) | async-done | bytes 131088 | tf_op jit(solution)/shard_map/reduce_scatter | solution.py:66
  (8 shorter events, 0.0 us)
Async XLA Ops:
  7.2 2.9 copy-start
  7.2 146.2 %all-reduce.7.cloned.1.call-start = ((), (), s32[]{:S(2)}) async-start(), calls=%async_computation.3 | async-start | bytes 163840
  8.2 1.9 copy-start.8
  8.5 0.9 copy-start.6
  9.4 0.6 copy-start.5
  10.0 232.4 %all-gather.2.cloned.1.call-start = ((), (), s32[]{:S(2)}) async-start(), calls=%async_computation.1 | async-start | bytes 21135360 | tf_op jit(solution)/shard_map/all_gather | solution.py:30
  11.5 5.4 copy-start.1
  11.5 6.2 copy-start.9
  11.5 230.9 %copy-start.10 = (s32[80]{0:T(128)S(1)}, s32[80]{0:T(128)}, u32[]{:S(2)}) copy-start(s32[80]{0:T(128)} %param.6) | copy-start | bytes 964
  17.6 990.6 %reduce-scatter.2.cloned.1.call-start = ((), (), s32[]{:S(2)}) async-start(), calls=%async_computation.2 | async-start | bytes 16908288 | tf_op jit(solution)/shard_map/reduce_scatter | solution.py:66
  321.1 14.9 %copy-start.2 = (bf16[80,4096]{1,0:T(8,128)(2,1)S(1)}, bf16[80,4096]{1,0:T(8,128)(2,1)}, u32[]{:S(2)}) copy-start(bf16[80,4096]{1,0:T(8,128)(2,1)} %copy-done.1) | copy-start | bytes 1966084
  335.4 0.7 copy-start.3
  344.1 1.4 copy-start.4
  344.1 1.4 copy-start.7
Sparse Core Ops, SparseCore 0:
  13.6 139.7 all-reduce.6
  156.8 85.6 all-gather.1
  344.3 663.9 reduce-scatter.1
where the time goes:
time: 1020 us
  waiting for transfers between devices  877 us (86%)
  blocking collectives  65.5 us (6%)
  matrix products  49.8 us (5%)
  between operations  16.5 us (2%)
    reduce_scatter x1, waiting for transfers between devices, local(): lax.psum_scatter(lax.dot_general(pooled, embed_grad, (((0,), (0,)), ((),...  654 us
    unnamed x4, waiting for transfers between devices  136 us
    all_gather x1, waiting for transfers between devices, local(): lax.all_gather(unit_b, ('dp', 'rep'), axis=0, tiled=True)  87.7 us
    unnamed x1, blocking collectives  65.5 us
  transfers between devices with their start and end apart: 3, of which 3 were waited for; matrix products, arithmetic and copies ran while one was open for 2% of the time, Pallas kernels for 0%

commit v1 on v0

v1 whole, which is shorter than its diff:
```python
import functools
import math

import jax
import jax.numpy as jnp
from jax import lax
from jax.experimental import pallas as pl
from jax.experimental.pallas import tpu as pltpu
from jax.sharding import PartitionSpec as P

MESH = pl.DeviceIdType.MESH
F32 = jnp.float32
BF16 = jnp.bfloat16
CAP = 80
TOK = 384
D = 4096
F = 1024
ROWS = 640
COLS = 1280
EXTRA = COLS + 128
MULT = 1.0 / (0.3 * math.sqrt(F))
LOG2E = 1.4426950408889634
NEG = -1e30
MARK = 256.0


def rcopy(src, dst, send_sem, recv_sem, device):
    return pltpu.make_async_remote_copy(
        src_ref=src, dst_ref=dst, send_sem=send_sem, recv_sem=recv_sem, device_id=device, device_id_type=MESH
    )


class GatherDp:
    def __init__(self, buf, ssem, rsem, z, y, rep):
        self.buf, self.ssem, self.rsem = buf, ssem, rsem
        self.z = [z, (z + 1) % 4, (z + 2) % 4, (z + 3) % 4]
        self.y = [y, (y + 1) % 4, (y + 2) % 4, (y + 3) % 4]
        self.dev = [
            (self.z[1] * 4 + y, rep),
            (self.z[3] * 4 + y, rep),
            (z * 4 + self.y[1], rep),
            (z * 4 + self.y[3], rep),
        ]
        self.copies = {}

    def send(self, direction, slot, h, d, dz, dy):
        at = pl.ds(pl.multiple_of((self.z[dz % 4] * 4 + self.y[dy % 4]) * CAP, CAP), CAP)
        piece = self.buf.at[h, d, at]
        c = rcopy(piece, piece, self.ssem.at[direction, slot], self.rsem.at[direction, slot], self.dev[direction])
        c.start()
        self.copies[direction, slot] = c

    def recv(self, *which):
        for w in which:
            self.copies[w].wait_recv()

    def round1(self):
        a = slice(None)
        for direction in range(4):
            self.send(direction, 0, a, a, 0, 0)

    def round2(self):
        a = slice(None)
        self.recv((0, 0))
        self.send(0, 1, a, 0, -1, 0)
        self.send(2, 2, 0, a, -1, 0)
        self.send(3, 2, 0, a, -1, 0)
        self.recv((2, 0))
        self.send(2, 1, a, 0, 0, -1)
        self.send(0, 2, 1, a, 0, -1)
        self.send(1, 2, 1, a, 0, -1)
        self.recv((1, 0))
        self.send(1, 1, a, 1, 1, 0)
        self.send(2, 3, 0, a, 1, 0)
        self.send(3, 3, 0, a, 1, 0)
        self.recv((3, 0))
        self.send(3, 1, a, 1, 0, 1)
        self.send(0, 3, 1, a, 0, 1)
        self.send(1, 3, 1, a, 0, 1)

    def round3(self):
        a = slice(None)
        self.recv((0, 1), (1, 1))
        self.send(2, 4, 0, a, 2, 0)
        self.send(3, 4, 0, a, 2, 0)
        self.recv((2, 1), (3, 1))
        self.send(0, 4, 1, a, 0, 2)
        self.send(1, 4, 1, a, 0, 2)
        self.recv((0, 2))
        self.send(0, 5, 1, 0, -1, -1)
        self.recv((2, 2))
        self.send(2, 5, 0, 0, -1, -1)
        self.recv((1, 2))
        self.send(1, 5, 1, 1, 1, -1)
        self.recv((3, 2))
        self.send(3, 5, 0, 1, -1, 1)
        self.recv((0, 3))
        self.send(0, 6, 1, 0, -1, 1)
        self.recv((2, 3))
        self.send(2, 6, 0, 0, 1, -1)
        self.recv((1, 3))
        self.send(1, 6, 1, 1, 1, 1)
        self.recv((3, 3))
        self.send(3, 6, 0, 1, 1, 1)

    def round4(self):
        self.recv((0, 4))
        self.send(0, 7, 1, 0, -1, 2)
        self.recv((1, 4))
        self.send(1, 7, 1, 1, 1, 2)
        self.recv((2, 4))
        self.send(2, 7, 0, 0, 2, -1)
        self.recv((3, 4))
        self.send(3, 7, 0, 1, 2, 1)

    def finish(self):
        for slot in (5, 6, 7):
            for direction in range(4):
                self.recv((direction, slot))

    def drain(self):
        for c in self.copies.values():
            c.wait_send()


class GatherRep:
    def __init__(self, buf, ssem, rsem, dp, x, k):
        self.buf, self.ssem, self.rsem, self.k = buf, ssem, rsem, k
        self.x = [x, (x + 1) % 4, (x + 2) % 4, (x + 3) % 4]
        self.dev = [(dp, self.x[1] * 2 + k), (dp, self.x[3] * 2 + k), (dp, x * 2 + 1 - k)]
        self.copies = {}

    def send(self, direction, slot, u, dx):
        at = pl.ds(pl.multiple_of((self.x[dx % 4] * 2 + self.k) * CAP, CAP), CAP)
        piece = self.buf.at[u, :, at]
        c = rcopy(piece, piece, self.ssem.at[direction, slot], self.rsem.at[direction, slot], self.dev[direction])
        c.start()
        self.copies[direction, slot] = c

    def recv(self, *which):
        for w in which:
            self.copies[w].wait_recv()

    def round1(self):
        for direction in range(3):
            self.send(direction, 0, slice(None), 0)

    def round2(self):
        self.recv((0, 0))
        self.send(0, 1, 0, -1)
        self.send(2, 1, slice(None), -1)
        self.recv((1, 0))
        self.send(1, 1, 1, 1)
        self.send(2, 2, slice(None), 1)

    def round3(self):
        self.recv((0, 1))
        self.send(2, 3, 0, 2)
        self.recv((1, 1))
        self.send(2, 4, 1, 2)

    def finish(self):
        for slot in range(5):
            self.recv((2, slot))

    def drain(self):
        for c in self.copies.values():
            c.wait_send()


class ReduceRep:
    def __init__(self, full, out, sib, far, far_in, near, near_in, mid, mid_in, ssem, rsem, dp, x, k):
        self.full, self.out, self.sib = full, out, sib
        self.far, self.far_in, self.near, self.near_in, self.mid, self.mid_in = far, far_in, near, near_in, mid, mid_in
        self.ssem, self.rsem, self.k = ssem, rsem, k
        self.x = [x, (x + 1) % 4, (x + 2) % 4, (x + 3) % 4]
        self.right, self.left = (dp, self.x[1] * 2 + k), (dp, self.x[3] * 2 + k)
        self.other = (dp, x * 2 + 1 - k)
        self.copies = {}

    def send(self, kind, q, src, dst, device):
        c = rcopy(src, dst, self.ssem.at[kind, q], self.rsem.at[kind, q], device)
        c.start()
        self.copies[kind, q] = c

    def put(self, q, value):
        parts = value.reshape((4, 2) + (value.shape[0] // 8, 256))
        self.full[q] = parts
        self.out[q] = parts.astype(self.out.dtype)
        self.send(0, q, self.out.at[q, :, 1 - self.k], self.sib.at[q], self.other)

    def part(self, q, dx):
        at = self.x[dx % 4]
        return self.full[q, at, self.k] + self.sib[q, at].astype(F32)

    def step1(self, q):
        self.copies[0, q].wait_recv()
        ahead, behind = (self.right, self.left) if q < 2 else (self.left, self.right)
        self.far[q] = self.part(q, 2).astype(self.far.dtype)
        self.send(1, q, self.far.at[q], self.far_in.at[q], ahead)
        self.near[q] = self.part(q, -1 if q < 2 else 1).astype(self.near.dtype)
        self.send(2, q, self.near.at[q], self.near_in.at[q], behind)

    def step2(self, q):
        self.copies[1, q].wait_recv()
        self.mid[q] = (self.part(q, 1 if q < 2 else -1) + self.far_in[q].astype(F32)).astype(self.mid.dtype)
        self.send(3, q, self.mid.at[q], self.mid_in.at[q], self.right if q < 2 else self.left)

    def result(self, q):
        self.copies[2, q].wait_recv()
        self.copies[3, q].wait_recv()
        return self.part(q, 0) + self.near_in[q].astype(F32) + self.mid_in[q].astype(F32)

    def drain(self):
        for c in self.copies.values():
            c.wait_send()


ORDER = (0, 2, 1, 3)


def kernel(
    hidden_hbm, slot_ref, pos_ref, proj_hbm,
    pgrad_out, proj_out, loss_out,
    hid, proj, pooled, pooled_in, pooled_t, uc, ur, ec, scores, weights, rowsum, zc, zr, zl, bias_c,
    posterm, unit_s,
    g_full, g_out, g_sib, g_far, g_far_in, g_near, g_near_in, g_mid, g_mid_in,
    p_full, p_out, p_sib, p_far, p_far_in, p_near, p_near_in, p_mid, p_mid_in,
    load_sem, uc_s, uc_r, ur_s, ur_r, ec_s, ec_r, g_s, g_r, p_s, p_r, a2a_s, a2a_r, zc_s, zc_r, zr_s, zr_r, zl_s, zl_r,
):
    dp, rep = lax.axis_index("dp"), lax.axis_index("rep")
    z, y, x, k = dp // 4, dp % 4, rep // 2, rep % 2
    dp_peers = [((dp + j) % 16, rep) for j in range(1, 16)]
    rep_peers = [(dp, (rep + j) % 8) for j in range(1, 8)]

    loads = []
    for j in range(4):
        loads.append(
            (
                pltpu.make_async_copy(hidden_hbm.at[:, pl.ds(j * 1024, 1024)], hid.at[j], load_sem.at[0, j]),
                pltpu.make_async_copy(proj_hbm.at[pl.ds(j * 1024, 1024)], proj.at[pl.ds(j * 1024, 1024)], load_sem.at[1, j]),
            )
        )
        loads[-1][0].start()
        loads[-1][1].start()

    barrier = pltpu.get_barrier_semaphore()
    for peer in dp_peers + rep_peers:
        pl.semaphore_signal(barrier, inc=1, device_id=peer, device_id_type=MESH)

    member = slot_ref[...] == lax.broadcasted_iota(jnp.int32, (CAP, TOK), 0)
    onehot = member.astype(F32)
    counts = jnp.sum(onehot, axis=1, keepdims=True)
    onehot = onehot.astype(BF16)
    denom = jnp.maximum(counts, 1.0)
    live = counts > 0.0
    embed = jnp.zeros((CAP, F), F32)
    for j in range(4):
        loads[j][0].wait()
        chunk = (jnp.dot(onehot, hid[j], preferred_element_type=F32) / denom).astype(BF16)
        for i in range(4):
            pooled[j * 4 + i] = chunk[:, i * 256 : (i + 1) * 256]
        loads[j][1].wait()
        embed = embed + jnp.dot(chunk, proj[pl.ds(j * 1024, 1024), :], preferred_element_type=F32)
    rscale = lax.rsqrt(jnp.mean(embed * embed, axis=1, keepdims=True) + 1e-06)
    unit = embed * rscale
    unit_s[...] = unit
    unit_b = unit.astype(BF16)
    lane = lax.broadcasted_iota(jnp.int32, (CAP, F), 1)
    marked = jnp.where(jnp.logical_and(lane == 0, jnp.logical_not(live)), MARK, unit).astype(BF16)
    at_c = pl.ds(pl.multiple_of(dp * CAP, CAP), CAP)
    at_r = pl.ds(pl.multiple_of(rep * CAP, CAP), CAP)
    for q in range(4):
        piece = marked[:, q * 256 : (q + 1) * 256]
        uc[q // 2, q % 2, at_c, :] = piece
        ur[q // 2, q % 2, at_r, :] = piece

    pl.semaphore_wait(barrier, 22)

    gc = GatherDp(uc, uc_s, uc_r, z, y, rep)
    gr = GatherRep(ur, ur_s, ur_r, dp, x, k)
    gc.round1()
    gr.round1()

    at_pos = pos_ref[...] - (dp * 8 + rep) * CAP
    row80 = lax.broadcasted_iota(jnp.int32, (CAP, CAP), 0)
    col80 = lax.broadcasted_iota(jnp.int32, (CAP, CAP), 1)
    back = jnp.where(jnp.logical_and(at_pos == row80, row80 != col80), 1.0, 0.0).astype(BF16)
    partner = lax.dot_general(back, unit_b, (((0,), (0,)), ((), ())), preferred_element_type=F32)
    posterm[...] = partner + jnp.dot(back, unit_b, preferred_element_type=F32)
    picked = jnp.sum(jnp.sum(partner * unit_b.astype(F32), axis=1, keepdims=True), axis=0, keepdims=True) * MULT

    gr.round2()
    gc.round2()
    gr.round3()
    gc.round3()
    gc.round4()
    gr.finish()
    gc.finish()

    a2a = []
    for j in range(15):
        peer = dp_peers[j]
        c = rcopy(pooled.at[peer[0]], pooled_in.at[pl.ds(pl.multiple_of(dp * CAP, CAP), CAP)], a2a_s.at[j], a2a_r.at[j], peer)
        c.start()
        a2a.append(c)
    pooled_in[at_c, :] = pooled[dp]

    rows = jnp.concatenate([ur[q // 2, q % 2] for q in range(4)], axis=1)
    live_r = ur[0, 0, :, 0:1].astype(F32) < 128.0
    bias_r = jnp.where(live_r, 0.0, NEG)
    nlive_r = jnp.sum(jnp.where(live_r, 1.0, 0.0), axis=0, keepdims=True)
    id_r = lax.broadcasted_iota(jnp.int32, (ROWS, 1), 0) - rep * CAP
    id_r = jnp.where(jnp.logical_and(id_r >= 0, id_r < CAP), id_r, -1)
    pick0 = jnp.where(lax.broadcasted_iota(jnp.int32, (16, 256), 1) == 0, 1.0, 0.0).astype(BF16)
    rowsum[...] = jnp.zeros_like(rowsum)

    def score_tile(t, carry):
        at = pl.ds(pl.multiple_of(t * 256, 256), 256)
        cols = jnp.concatenate([uc[q // 2, q % 2, at, :] for q in range(4)], axis=1)
        first = lax.dot_general(pick0, cols[:, :256], (((1,), (1,)), ((), ())), preferred_element_type=F32)
        bias = jnp.where(first[0:1] < 128.0, 0.0, NEG)
        bias_c[:, at] = bias
        id_c = lax.broadcasted_iota(jnp.int32, (1, 256), 1) + t * 256 - dp * CAP
        id_c = jnp.where(jnp.logical_and(id_c >= 0, id_c < CAP), id_c, -2)
        s = lax.dot_general(rows, cols, (((1,), (1,)), ((), ())), preferred_element_type=F32) * (MULT * LOG2E)
        s = jnp.where(id_r == id_c, NEG, s + bias_r + bias)
        scores[:, at] = s
        e = jnp.exp2(s)
        zc[dp, :, at] = jnp.sum(e, axis=0, keepdims=True)
        rowsum[...] += e[:, :128] + e[:, 128:]
        return carry

    lax.fori_loop(0, 5, score_tile, 0)
    zr[rep] = jnp.sum(rowsum[...].T, axis=0, keepdims=True)
    l128 = lax.broadcasted_iota(jnp.int32, (1, 128), 1)
    zc[dp, :, pl.ds(COLS, 128)] = jnp.where(l128 == 0, nlive_r, jnp.where(l128 == 1, picked, 0.0))

    zcopies = []
    for j in range(15):
        zcopies.append(rcopy(zc.at[dp], zc.at[dp], zc_s.at[j], zc_r.at[j], dp_peers[j]))
        zcopies[-1].start()
    for j in range(7):
        zcopies.append(rcopy(zr.at[rep], zr.at[rep], zr_s.at[j], zr_r.at[j], rep_peers[j]))
        zcopies[-1].start()
    for c in zcopies:
        c.wait_recv()

    total_c = zc[0]
    for j in range(1, 16):
        total_c = total_c + zc[j]
    total_r = zr[0]
    for j in range(1, 8):
        total_r = total_r + zr[j]
    nlive = total_c[:, COLS : COLS + 1]
    log_c = jnp.where(bias_c[...] < -1.0, 0.0, jnp.log(total_c[:, :COLS]))
    loss_c = jnp.sum(log_c, axis=1, keepdims=True) - total_c[:, COLS + 1 : COLS + 2]
    zl[rep] = jnp.broadcast_to(loss_c, (1, 128))
    lcopies = []
    for j in range(7):
        lcopies.append(rcopy(zl.at[rep], zl.at[rep], zl_s.at[j], zl_r.at[j], rep_peers[j]))
        lcopies[-1].start()
    bias_c[...] = log_c * LOG2E
    log_r = jnp.broadcast_to(jnp.log(total_r) * LOG2E, (128, ROWS)).T
    log_r = jnp.where(live_r, log_r, 0.0)
    rowsum[...] = log_r

    def weight_tile(t, carry):
        at = pl.ds(pl.multiple_of(t * 128, 128), 128)
        s = scores[:, at]
        w = jnp.exp2(s - rowsum[...]) + jnp.exp2(s - bias_c[:, at])
        weights[:, at] = w.astype(BF16)
        return carry

    lax.fori_loop(0, 10, weight_tile, 0)

    red = ReduceRep(g_full, g_out, g_sib, g_far, g_far_in, g_near, g_near_in, g_mid, g_mid_in, g_s, g_r, dp, x, k)
    for q in ORDER:
        red.put(q, jnp.dot(weights[...], uc[q // 2, q % 2], preferred_element_type=F32))
    for q in ORDER:
        red.step1(q)
    for q in ORDER:
        red.step2(q)
    got = jnp.concatenate([red.result(q) for q in range(4)], axis=1)
    unit = unit_s[...]
    ugrad = (got - posterm[...]) * (MULT / nlive)
    inner = jnp.mean(unit * ugrad, axis=1, keepdims=True)
    egrad = (rscale * (ugrad - unit * inner)).astype(BF16)
    for q in range(4):
        ec[q // 2, q % 2, at_c, :] = egrad[:, q * 256 : (q + 1) * 256]

    ge = GatherDp(ec, ec_s, ec_r, z, y, rep)

    def pgrad(j):
        at = pl.ds(j * 512, 512)
        part = lax.dot_general(egrad, proj[at, :], (((1,), (1,)), ((), ())), preferred_element_type=F32)
        pgrad_out[:, at] = (part / denom).astype(BF16)

    ge.round1()
    for c in a2a:
        c.wait_recv()
    pooled_t[...] = pooled_in[...].astype(F32).T.astype(BF16)
    pgrad(0)
    ge.round2()
    pgrad(1)
    pgrad(2)
    ge.round3()
    pgrad(3)
    pgrad(4)
    ge.round4()
    for j in range(5, 8):
        pgrad(j)
    ge.finish()

    red2 = ReduceRep(p_full, p_out, p_sib, p_far, p_far_in, p_near, p_near_in, p_mid, p_mid_in, p_s, p_r, dp, x, k)
    for q in ORDER:
        red2.put(q, jnp.dot(pooled_t[...], ec[q // 2, q % 2], preferred_element_type=F32))
    for q in ORDER:
        red2.step1(q)
    for q in ORDER:
        red2.step2(q)
    for q in range(4):
        proj_out[:, q * 256 : (q + 1) * 256] = red2.result(q)

    for c in lcopies:
        c.wait_recv()
    loss = zl[0]
    for j in range(1, 8):
        loss = loss + zl[j]
    loss_out[...] = loss / nlive

    for group in (gc, gr, red, ge, red2):
        group.drain()
    for c in a2a + zcopies + lcopies:
        c.wait_send()


def reduce_scratch(n, kind):
    return [pltpu.VMEM((4, 4, 2, n, 256), F32), pltpu.VMEM((4, 4, 2, n, 256), kind), pltpu.VMEM((4, 4, n, 256), kind)] + [
        pltpu.VMEM((4, n, 256), kind) for _ in range(6)
    ]


def local(hidden, step_slot, positive, proj):
    dma = pltpu.SemaphoreType.DMA
    vm = pl.BlockSpec(memory_space=pltpu.VMEM)
    hbm = pl.BlockSpec(memory_space=pl.ANY)
    pooled_grad, proj_grad, loss = pl.pallas_call(
        kernel,
        out_shape=(
            jax.ShapeDtypeStruct((CAP, D), BF16),
            jax.ShapeDtypeStruct((32, F), F32),
            jax.ShapeDtypeStruct((1, 128), F32),
        ),
        in_specs=[hbm, vm, vm, hbm],
        out_specs=(vm, vm, vm),
        scratch_shapes=[
            pltpu.VMEM((4, TOK, 1024), BF16),
            pltpu.VMEM((D, F), BF16),
            pltpu.VMEM((16, CAP, 256), BF16),
            pltpu.VMEM((COLS, 256), BF16),
            pltpu.VMEM((256, COLS), BF16),
            pltpu.VMEM((2, 2, COLS, 256), BF16),
            pltpu.VMEM((2, 2, ROWS, 256), BF16),
            pltpu.VMEM((2, 2, COLS, 256), BF16),
            pltpu.VMEM((ROWS, COLS), F32),
            pltpu.VMEM((ROWS, COLS), BF16),
            pltpu.VMEM((ROWS, 128), F32),
            pltpu.VMEM((16, 1, EXTRA), F32),
            pltpu.VMEM((8, 1, ROWS), F32),
            pltpu.VMEM((8, 1, 128), F32),
            pltpu.VMEM((1, COLS), F32),
            pltpu.VMEM((CAP, F), F32),
            pltpu.VMEM((CAP, F), F32),
        ]
        + reduce_scratch(CAP, BF16)
        + reduce_scratch(32, BF16)
        + [
            dma((2, 4)),
            dma((4, 8)), dma((4, 8)), dma((3, 5)), dma((3, 5)), dma((4, 8)), dma((4, 8)),
            dma((4, 4)), dma((4, 4)), dma((4, 4)), dma((4, 4)),
            dma((15,)), dma((15,)), dma((15,)), dma((15,)), dma((7,)), dma((7,)), dma((7,)), dma((7,)),
        ],
        compiler_params=pltpu.CompilerParams(
            collective_id=0, has_side_effects=True, vmem_limit_bytes=60 * 1024 * 1024
        ),
        cost_estimate=pl.CostEstimate(flops=6_000_000_000, bytes_accessed=14_000_000, transcendentals=2_000_000),
    )(hidden, step_slot.reshape(1, TOK), positive.reshape(1, CAP), proj)
    onehot = (step_slot[None, :] == lax.broadcasted_iota(jnp.int32, (CAP, TOK), 0)).astype(BF16)
    hidden_grad = lax.dot_general(onehot, pooled_grad, (((0,), (0,)), ((), ())), preferred_element_type=F32)
    return (hidden_grad.astype(BF16), proj_grad, loss[0, 0])


def solution(mesh):
    in_specs = (P(("dp", "rep"), None), P(("dp", "rep")), P(("dp", "rep")), P())
    out_specs = (P(("dp", "rep"), None), P(("dp", "rep"), None), P())
    return jax.shard_map(local, mesh=mesh, in_specs=in_specs, out_specs=out_specs, check_vma=False)
```

time: 1020 us -> 98.9 us (0.10)
  waiting for transfers between devices: 877 us -> 0 us
  Pallas kernels: 0 us -> 91.1 us
  blocking collectives: 65.5 us -> 0 us
  matrix products: 49.8 us -> 3.82 us
  between operations: 16.5 us -> 1.83 us
    reduce_scatter x1 -> x0, waiting for transfers between devices: 654 us -> none  [local(): lax.psum_scatter(lax.dot_general(pooled, embed_grad, (((0,), (0,)), ((),...]
    unnamed x4 -> x0, waiting for transfers between devices: 136 us -> none
    pallas_call x0 -> x1, Pallas kernels: none -> 91.1 us  [local(): pl.pallas_call(kernel, out_shape=(jax.ShapeDtypeStruct((CAP, D), BF16), j...]
    all_gather x1 -> x0, waiting for transfers between devices: 87.7 us -> none  [local(): lax.all_gather(unit_b, ('dp', 'rep'), axis=0, tiled=True)]
    unnamed x1 -> x0, blocking collectives: 65.5 us -> none
    dot_general x5 -> x0, matrix products: 41.3 us -> none  [the longest x1 14.1 us: local(): jnp.dot(weights, all_unit, preferred_element_type=jnp.float32)]
  transfers between devices with their start and end apart: 3 -> 0, of which waited for: 3 -> 0; matrix products, arithmetic and copies ran while one was open for 2% -> 0% of each run, Pallas kernels for 0% -> 0%
where the time goes in v1:
time: 98.9 us; the launch traced here: 98.7 us
  Pallas kernels  91.1 us (92%)
  matrix products  3.82 us (4%)
  local copies, waits for them, and re-layouts  1.91 us (2%)
  between operations  1.83 us (2%)
    pallas_call x1, Pallas kernels, local(): pl.pallas_call(kernel, out_shape=(jax.ShapeDtypeStruct((CAP, D), BF16), j...  91.1 us
    dot_general x1, matrix products, local(): lax.dot_general(onehot, pooled_grad, (((0,), (0,)), ((), ())), preferred_...  3.82 us

profile of v1, /device:TPU:0, one launch (start us, length us, event | category | flops | bytes accessed | tf_op | source)
XLA Modules:
  0.0 98.7 jit_solution(18267436222295329842)
XLA Ops:
  0.6 1.2 %broadcast_in_dim.3.slot_ref = s32[1,384]{1,0:T(1,128)} reshape(s32[384]{0:T(512)} %param.5) | data formatting | bytes 3072 | tf_op jit(solution)/shard_map/broadcast_in_dim | solution.py:489
  1.9 0.0 copy-start.1
  1.9 91.1 %shard_map.67 = (bf16[80,4096]{1,0:T(8,128)(2,1)}, f32[32,1024]{1,0:T(8,128)}, f32[1,128]{1,0:T(1,128)}) custom-call(bf16[384,4096]{1,0:T(8,128)(2,1)} %hidden_hbm.1, s32[1,384]{1,0:T(1,128)} %broadcast_in_dim.3.slot_ref, s32[1,80]{1,0:T(1,128)} %bitcast.4, bf16[4096,1024]{1,0:T(8,128)(2,1)} %proj_hbm.1), custom_call_target="tpu_custom_call" | custom-call | flops 6000000000 | bytes 14000000 | tf_op jit(solution)/shard_map/pallas_call | solution.py:448
  93.0 0.0 copy-start
  93.0 0.0 copy-start.2
  93.1 0.0 copy-done.1
  93.1 3.8 %convolution_convert_fusion = bf16[384,4096]{1,0:T(8,128)(2,1)} fusion(bf16[80,4096]{1,0:T(8,128)(2,1)} %get-tuple-element.6, s32[384]{0:T(512)S(1)} %copy-done.1), kind=kOutput, calls=%fused_computation | convolution fusion | flops 253261824 | bytes 3802624 | tf_op jit(solution)/shard_map/dot_general | solution.py:490
  96.9 0.0 copy-done
  96.9 0.7 copy.9
  97.5 0.0 copy-done.2
Async XLA Ops:
  1.9 91.2 %copy-start.1 = (s32[384]{0:T(512)S(1)}, s32[384]{0:T(512)}, u32[]{:S(2)}) copy-start(s32[384]{0:T(512)} %param.5) | copy-start | bytes 4612
  93.0 3.8 %copy-start = (f32[32,1024]{1,0:T(8,128)S(1)}, f32[32,1024]{1,0:T(8,128)}, u32[]{:S(2)}) copy-start(f32[32,1024]{1,0:T(8,128)} %get-tuple-element.13) | copy-start | bytes 393220
  93.0 4.5 %copy-start.2 = (f32[1,128]{1,0:T(1,128)S(1)}, f32[1,128]{1,0:T(1,128)}, u32[]{:S(2)}) copy-start(f32[1,128]{1,0:T(1,128)} %get-tuple-element.8) | copy-start | bytes 1540

commit v2 on v1

--- a/solution.py
+++ b/solution.py
@@ -43,9 +43,11 @@
         ]
         self.copies = {}
 
+    def at(self, dz, dy):
+        return pl.ds(pl.multiple_of((self.z[dz % 4] * 4 + self.y[dy % 4]) * CAP, CAP), CAP)
+
     def send(self, direction, slot, h, d, dz, dy):
-        at = pl.ds(pl.multiple_of((self.z[dz % 4] * 4 + self.y[dy % 4]) * CAP, CAP), CAP)
-        piece = self.buf.at[h, d, at]
+        piece = self.buf.at[h, d, self.at(dz, dy)]
         c = rcopy(piece, piece, self.ssem.at[direction, slot], self.rsem.at[direction, slot], self.dev[direction])
         c.start()
         self.copies[direction, slot] = c
@@ -54,69 +56,88 @@
         for w in which:
             self.copies[w].wait_recv()
 
-    def round1(self):
+    def start(self, h):
         a = slice(None)
-        for direction in range(4):
-            self.send(direction, 0, a, a, 0, 0)
-
-    def round2(self):
+        for direction in (0, 1) if h == 0 else (2, 3):
+            self.send(direction, 0, h, a, 0, 0)
+        for direction in (2, 3) if h == 0 else (0, 1):
+            self.send(direction, 8, h, a, 0, 0)
+
+    def first(self, h):
         a = slice(None)
-        self.recv((0, 0))
-        self.send(0, 1, a, 0, -1, 0)
-        self.send(2, 2, 0, a, -1, 0)
-        self.send(3, 2, 0, a, -1, 0)
-        self.recv((2, 0))
-        self.send(2, 1, a, 0, 0, -1)
-        self.send(0, 2, 1, a, 0, -1)
-        self.send(1, 2, 1, a, 0, -1)
-        self.recv((1, 0))
-        self.send(1, 1, a, 1, 1, 0)
-        self.send(2, 3, 0, a, 1, 0)
-        self.send(3, 3, 0, a, 1, 0)
-        self.recv((3, 0))
-        self.send(3, 1, a, 1, 0, 1)
-        self.send(0, 3, 1, a, 0, 1)
-        self.send(1, 3, 1, a, 0, 1)
-
-    def round3(self):
+        if h == 0:
+            self.recv((0, 0))
+            self.send(0, 1, 0, 0, -1, 0)
+            self.send(2, 2, 0, a, -1, 0)
+            self.send(3, 2, 0, a, -1, 0)
+            self.recv((1, 0))
+            self.send(1, 1, 0, 1, 1, 0)
+            self.send(2, 3, 0, a, 1, 0)
+            self.send(3, 3, 0, a, 1, 0)
+        else:
+            self.recv((2, 0))
+            self.send(2, 1, 1, 0, 0, -1)
+            self.send(0, 2, 1, a, 0, -1)
+            self.send(1, 2, 1, a, 0, -1)
+            self.recv((3, 0))
+            self.send(3, 1, 1, 1, 0, 1)
+            self.send(0, 3, 1, a, 0, 1)
+            self.send(1, 3, 1, a, 0, 1)
+
+    def second(self, h):
+        if h == 0:
+            self.recv((2, 8))
+            self.send(2, 9, 0, 0, 0, -1)
+            self.recv((3, 8))
+            self.send(3, 9, 0, 1, 0, 1)
+        else:
+            self.recv((0, 8))
+            self.send(0, 9, 1, 0, -1, 0)
+            self.recv((1, 8))
+            self.send(1, 9, 1, 1, 1, 0)
+
+    def far(self, h):
         a = slice(None)
-        self.recv((0, 1), (1, 1))
-        self.send(2, 4, 0, a, 2, 0)
-        self.send(3, 4, 0, a, 2, 0)
-        self.recv((2, 1), (3, 1))
-        self.send(0, 4, 1, a, 0, 2)
-        self.send(1, 4, 1, a, 0, 2)
-        self.recv((0, 2))
-        self.send(0, 5, 1, 0, -1, -1)
-        self.recv((2, 2))
-        self.send(2, 5, 0, 0, -1, -1)
-        self.recv((1, 2))
-        self.send(1, 5, 1, 1, 1, -1)
-        self.recv((3, 2))
-        self.send(3, 5, 0, 1, -1, 1)
-        self.recv((0, 3))
-        self.send(0, 6, 1, 0, -1, 1)
-        self.recv((2, 3))
-        self.send(2, 6, 0, 0, 1, -1)
-        self.recv((1, 3))
-        self.send(1, 6, 1, 1, 1, 1)
-        self.recv((3, 3))
-        self.send(3, 6, 0, 1, 1, 1)
-
-    def round4(self):
-        self.recv((0, 4))
-        self.send(0, 7, 1, 0, -1, 2)
-        self.recv((1, 4))
-        self.send(1, 7, 1, 1, 1, 2)
-        self.recv((2, 4))
-        self.send(2, 7, 0, 0, 2, -1)
-        self.recv((3, 4))
-        self.send(3, 7, 0, 1, 2, 1)
-
-    def finish(self):
-        for slot in (5, 6, 7):
-            for direction in range(4):
-                self.recv((direction, slot))
+        if h == 0:
+            self.recv((0, 1), (1, 1))
+            self.send(2, 4, 0, a, 2, 0)
+            self.send(3, 4, 0, a, 2, 0)
+        else:
+            self.recv((2, 1), (3, 1))
+            self.send(0, 4, 1, a, 0, 2)
+            self.send(1, 4, 1, a, 0, 2)
+
+    def cross(self, h):
+        if h == 0:
+            self.recv((2, 2))
+            self.send(2, 5, 0, 0, -1, -1)
+            self.recv((3, 2))
+            self.send(3, 5, 0, 1, -1, 1)
+            self.recv((2, 3))
+            self.send(2, 6, 0, 0, 1, -1)
+            self.recv((3, 3))
+            self.send(3, 6, 0, 1, 1, 1)
+        else:
+            self.recv((0, 2))
+            self.send(0, 5, 1, 0, -1, -1)
+            self.recv((1, 2))
+            self.send(1, 5, 1, 1, 1, -1)
+            self.recv((0, 3))
+            self.send(0, 6, 1, 0, -1, 1)
+            self.recv((1, 3))
+            self.send(1, 6, 1, 1, 1, 1)
+
+    def last(self, h):
+        if h == 0:
+            self.recv((2, 4))
+            self.send(2, 7, 0, 0, 2, -1)
+            self.recv((3, 4))
+            self.send(3, 7, 0, 1, 2, 1)
+        else:
+            self.recv((0, 4))
+            self.send(0, 7, 1, 0, -1, 2)
+            self.recv((1, 4))
+            self.send(1, 7, 1, 1, 1, 2)
 
     def drain(self):
         for c in self.copies.values():
@@ -222,7 +243,7 @@
 def kernel(
     hidden_hbm, slot_ref, pos_ref, proj_hbm,
     pgrad_out, proj_out, loss_out,
-    hid, proj, pooled, pooled_in, pooled_t, uc, ur, ec, scores, weights, rowsum, zc, zr, zl, bias_c,
+    hid, proj, pooled, pooled_in, pooled_t, uc, ur, ec, scores, weights, rowsum, colpart, zc, zr, zl, bias_c,
     posterm, unit_s,
     g_full, g_out, g_sib, g_far, g_far_in, g_near, g_near_in, g_mid, g_mid_in,
     p_full, p_out, p_sib, p_far, p_far_in, p_near, p_near_in, p_mid, p_mid_in,
@@ -245,7 +266,9 @@
         loads[-1][1].start()
 
     barrier = pltpu.get_barrier_semaphore()
-    for peer in dp_peers + rep_peers:
+    near = [((z + 1) % 4 * 4 + y, rep), ((z + 3) % 4 * 4 + y, rep), (z * 4 + (y + 1) % 4, rep), (z * 4 + (y + 3) % 4, rep)]
+    near += [(dp, (x + 1) % 4 * 2 + k), (dp, (x + 3) % 4 * 2 + k), (dp, x * 2 + 1 - k)]
+    for peer in near:
         pl.semaphore_signal(barrier, inc=1, device_id=peer, device_id_type=MESH)
 
     member = slot_ref[...] == lax.broadcasted_iota(jnp.int32, (CAP, TOK), 0)
@@ -275,11 +298,12 @@
         uc[q // 2, q % 2, at_c, :] = piece
         ur[q // 2, q % 2, at_r, :] = piece
 
-    pl.semaphore_wait(barrier, 22)
+    pl.semaphore_wait(barrier, 7)
 
     gc = GatherDp(uc, uc_s, uc_r, z, y, rep)
     gr = GatherRep(ur, ur_s, ur_r, dp, x, k)
-    gc.round1()
+    gc.start(0)
+    gc.start(1)
     gr.round1()
 
     at_pos = pos_ref[...] - (dp * 8 + rep) * CAP
@@ -290,30 +314,79 @@
     posterm[...] = partner + jnp.dot(back, unit_b, preferred_element_type=F32)
     picked = jnp.sum(jnp.sum(partner * unit_b.astype(F32), axis=1, keepdims=True), axis=0, keepdims=True) * MULT
 
+    def pair_sums(blocks, own):
+        cols = jnp.concatenate(
+            [jnp.concatenate([uc[q // 2, q % 2, gc.at(*b), :] for q in range(4)], axis=1) for b in blocks], axis=0
+        )
+        bias = jnp.where(cols[:, 0:1].astype(F32) < 128.0, 0.0, NEG)
+        s = lax.dot_general(cols, rows, (((1,), (1,)), ((), ())), preferred_element_type=F32) * (MULT * LOG2E)
+        s = s + bias + bias_l
+        if own:
+            lane = lax.broadcasted_iota(jnp.int32, (CAP, ROWS), 1) - rep * CAP
+            s = jnp.where(lane == lax.broadcasted_iota(jnp.int32, (CAP, ROWS), 0), NEG, s)
+        e = jnp.exp2(s)
+        part = e[:, :128]
+        for i in range(1, 5):
+            part = part + e[:, i * 128 : (i + 1) * 128]
+        for i, b in enumerate(blocks):
+            colpart[gc.at(*b), :] = part[i * CAP : (i + 1) * CAP]
+        return jnp.sum(e, axis=0, keepdims=True)
+
+    gc.first(0)
+    gc.first(1)
     gr.round2()
-    gc.round2()
+    gc.far(0)
+    gc.far(1)
     gr.round3()
-    gc.round3()
-    gc.round4()
+    gc.second(0)
+    gc.second(1)
     gr.finish()
-    gc.finish()
+    rows = jnp.concatenate([ur[q // 2, q % 2] for q in range(4)], axis=1)
+    live_r = ur[0, 0, :, 0:1].astype(F32) < 128.0
+    bias_r = jnp.where(live_r, 0.0, NEG)
+    pick0 = jnp.where(lax.broadcasted_iota(jnp.int32, (16, 256), 1) == 0, 1.0, 0.0).astype(BF16)
+    first = lax.dot_general(pick0, ur[0, 0], (((1,), (1,)), ((), ())), preferred_element_type=F32)
+    bias_l = jnp.where(first[0:1] < 128.0, 0.0, NEG)
+    nlive_r = jnp.sum(jnp.where(bias_l < -1.0, 0.0, 1.0), axis=1, keepdims=True)
+    sum_r = pair_sums([(0, 0)], True)
+    gc.cross(0)
+    gc.cross(1)
+    gc.last(0)
+    gc.last(1)
+    sum_r = sum_r + pair_sums([(-1, 0), (1, 0), (0, -1), (0, 1)], False)
+    for direction in range(4):
+        gc.recv((direction, 9))
+    sum_r = sum_r + pair_sums([(-1, -1), (-1, 1), (1, -1), (1, 1), (2, 0), (0, 2)], False)
+    for slot in (5, 6):
+        for direction in range(4):
+            gc.recv((direction, slot))
+    sum_r = sum_r + pair_sums([(-1, 2), (1, 2), (2, -1), (2, 1)], False)
+    for direction in range(4):
+        gc.recv((direction, 7))
+    sum_r = sum_r + pair_sums([(2, 2)], False)
+    zr[rep] = sum_r
+    zc[dp, :, pl.ds(0, COLS)] = jnp.sum(colpart[...].T, axis=0, keepdims=True)
+    l128 = lax.broadcasted_iota(jnp.int32, (1, 128), 1)
+    zc[dp, :, pl.ds(COLS, 128)] = jnp.where(l128 == 0, nlive_r, jnp.where(l128 == 1, picked, 0.0))
+
+    zcopies = []
+    for j in range(15):
+        zcopies.append(rcopy(zc.at[dp], zc.at[dp], zc_s.at[j], zc_r.at[j], dp_peers[j]))
+        zcopies[-1].start()
+    for j in range(7):
+        zcopies.append(rcopy(zr.at[rep], zr.at[rep], zr_s.at[j], zr_r.at[j], rep_peers[j]))
+        zcopies[-1].start()
 
     a2a = []
     for j in range(15):
         peer = dp_peers[j]
-        c = rcopy(pooled.at[peer[0]], pooled_in.at[pl.ds(pl.multiple_of(dp * CAP, CAP), CAP)], a2a_s.at[j], a2a_r.at[j], peer)
+        c = rcopy(pooled.at[peer[0]], pooled_in.at[at_c], a2a_s.at[j], a2a_r.at[j], peer)
         c.start()
         a2a.append(c)
     pooled_in[at_c, :] = pooled[dp]
 
-    rows = jnp.concatenate([ur[q // 2, q % 2] for q in range(4)], axis=1)
-    live_r = ur[0, 0, :, 0:1].astype(F32) < 128.0
-    bias_r = jnp.where(live_r, 0.0, NEG)
-    nlive_r = jnp.sum(jnp.where(live_r, 1.0, 0.0), axis=0, keepdims=True)
     id_r = lax.broadcasted_iota(jnp.int32, (ROWS, 1), 0) - rep * CAP
     id_r = jnp.where(jnp.logical_and(id_r >= 0, id_r < CAP), id_r, -1)
-    pick0 = jnp.where(lax.broadcasted_iota(jnp.int32, (16, 256), 1) == 0, 1.0, 0.0).astype(BF16)
-    rowsum[...] = jnp.zeros_like(rowsum)
 
     def score_tile(t, carry):
         at = pl.ds(pl.multiple_of(t * 256, 256), 256)
@@ -324,25 +397,10 @@
         id_c = lax.broadcasted_iota(jnp.int32, (1, 256), 1) + t * 256 - dp * CAP
         id_c = jnp.where(jnp.logical_and(id_c >= 0, id_c < CAP), id_c, -2)
         s = lax.dot_general(rows, cols, (((1,), (1,)), ((), ())), preferred_element_type=F32) * (MULT * LOG2E)
-        s = jnp.where(id_r == id_c, NEG, s + bias_r + bias)
-        scores[:, at] = s
-        e = jnp.exp2(s)
-        zc[dp, :, at] = jnp.sum(e, axis=0, keepdims=True)
-        rowsum[...] += e[:, :128] + e[:, 128:]
+        scores[:, at] = jnp.where(id_r == id_c, NEG, s + bias_r + bias)
         return carry
 
     lax.fori_loop(0, 5, score_tile, 0)
-    zr[rep] = jnp.sum(rowsum[...].T, axis=0, keepdims=True)
-    l128 = lax.broadcasted_iota(jnp.int32, (1, 128), 1)
-    zc[dp, :, pl.ds(COLS, 128)] = jnp.where(l128 == 0, nlive_r, jnp.where(l128 == 1, picked, 0.0))
-
-    zcopies = []
-    for j in range(15):
-        zcopies.append(rcopy(zc.at[dp], zc.at[dp], zc_s.at[j], zc_r.at[j], dp_peers[j]))
-        zcopies[-1].start()
-    for j in range(7):
-        zcopies.append(rcopy(zr.at[rep], zr.at[rep], zr_s.at[j], zr_r.at[j], rep_peers[j]))
-        zcopies[-1].start()
     for c in zcopies:
         c.wait_recv()
 
@@ -396,21 +454,30 @@
         part = lax.dot_general(egrad, proj[at, :], (((1,), (1,)), ((), ())), preferred_element_type=F32)
         pgrad_out[:, at] = (part / denom).astype(BF16)
 
-    ge.round1()
+    ge.start(0)
+    ge.start(1)
     for c in a2a:
         c.wait_recv()
     pooled_t[...] = pooled_in[...].astype(F32).T.astype(BF16)
+    ge.first(0)
+    ge.first(1)
     pgrad(0)
-    ge.round2()
+    ge.far(0)
+    ge.far(1)
+    ge.second(0)
+    ge.second(1)
     pgrad(1)
     pgrad(2)
-    ge.round3()
+    ge.cross(0)
+    ge.cross(1)
     pgrad(3)
-    pgrad(4)
-    ge.round4()
-    for j in range(5, 8):
+    ge.last(0)
+    ge.last(1)
+    for j in range(4, 8):
         pgrad(j)
-    ge.finish()
+    for slot in (9, 5, 6, 7):
+        for direction in range(4):
+            ge.recv((direction, slot))
 
     red2 = ReduceRep(p_full, p_out, p_sib, p_far, p_far_in, p_near, p_near_in, p_mid, p_mid_in, p_s, p_r, dp, x, k)
     for q in ORDER:
@@ -466,6 +533,7 @@
             pltpu.VMEM((ROWS, COLS), F32),
             pltpu.VMEM((ROWS, COLS), BF16),
             pltpu.VMEM((ROWS, 128), F32),
+            pltpu.VMEM((COLS, 128), F32),
             pltpu.VMEM((16, 1, EXTRA), F32),
             pltpu.VMEM((8, 1, ROWS), F32),
             pltpu.VMEM((8, 1, 128), F32),
@@ -477,7 +545,7 @@
         + reduce_scratch(32, BF16)
         + [
             dma((2, 4)),
-            dma((4, 8)), dma((4, 8)), dma((3, 5)), dma((3, 5)), dma((4, 8)), dma((4, 8)),
+            dma((4, 10)), dma((4, 10)), dma((3, 5)), dma((3, 5)), dma((4, 10)), dma((4, 10)),
             dma((4, 4)), dma((4, 4)), dma((4, 4)), dma((4, 4)),
             dma((15,)), dma((15,)), dma((15,)), dma((15,)), dma((7,)), dma((7,)), dma((7,)), dma((7,)),
         ],

time: 98.9 us -> 90.7 us (0.917)
  Pallas kernels: 91.1 us -> 83 us
    pallas_call x1, Pallas kernels: 91.1 us -> 83 us  [local(): pl.pallas_call(kernel, out_shape=(jax.ShapeDtypeStruct((CAP, D), BF16), j...]
where the time goes in v2:
time: 90.7 us; the launch traced here: 90.5 us
  Pallas kernels  83 us (92%)
  matrix products  3.81 us (4%)
  local copies, waits for them, and re-layouts  1.91 us (2%)
  between operations  1.83 us (2%)
    pallas_call x1, Pallas kernels, local(): pl.pallas_call(kernel, out_shape=(jax.ShapeDtypeStruct((CAP, D), BF16), j...  83 us
    dot_general x1, matrix products, local(): lax.dot_general(onehot, pooled_grad, (((0,), (0,)), ((), ())), preferred_...  3.81 us

profile of v2, /device:TPU:0, one launch (start us, length us, event | category | flops | bytes accessed | tf_op | source)
XLA Modules:
  0.0 90.5 jit_solution(17156514719763426837)
XLA Ops:
  0.6 1.2 %broadcast_in_dim.3.slot_ref = s32[1,384]{1,0:T(1,128)} reshape(s32[384]{0:T(512)} %param.5) | data formatting | bytes 3072 | tf_op jit(solution)/shard_map/broadcast_in_dim | solution.py:557
  1.9 0.0 copy-start.1
  1.9 83.0 %shard_map.67 = (bf16[80,4096]{1,0:T(8,128)(2,1)}, f32[32,1024]{1,0:T(8,128)}, f32[1,128]{1,0:T(1,128)}) custom-call(bf16[384,4096]{1,0:T(8,128)(2,1)} %hidden_hbm.1, s32[1,384]{1,0:T(1,128)} %broadcast_in_dim.3.slot_ref, s32[1,80]{1,0:T(1,128)} %bitcast.4, bf16[4096,1024]{1,0:T(8,128)(2,1)} %proj_hbm.1), custom_call_target="tpu_custom_call" | custom-call | flops 6000000000 | bytes 14000000 | tf_op jit(solution)/shard_map/pallas_call | solution.py:515
  84.8 0.0 copy-start
  84.9 0.0 copy-start.2
  84.9 0.0 copy-done.1
  84.9 3.8 %convolution_convert_fusion = bf16[384,4096]{1,0:T(8,128)(2,1)} fusion(bf16[80,4096]{1,0:T(8,128)(2,1)} %get-tuple-element.6, s32[384]{0:T(512)S(1)} %copy-done.1), kind=kOutput, calls=%fused_computation | convolution fusion | flops 253261824 | bytes 3802624 | tf_op jit(solution)/shard_map/dot_general | solution.py:558
  88.7 0.0 copy-done
  88.7 0.7 copy.9
  89.3 0.0 copy-done.2
Async XLA Ops:
  1.9 83.0 %copy-start.1 = (s32[384]{0:T(512)S(1)}, s32[384]{0:T(512)}, u32[]{:S(2)}) copy-start(s32[384]{0:T(512)} %param.5) | copy-start | bytes 4612
  84.8 3.8 %copy-start = (f32[32,1024]{1,0:T(8,128)S(1)}, f32[32,1024]{1,0:T(8,128)}, u32[]{:S(2)}) copy-start(f32[32,1024]{1,0:T(8,128)} %get-tuple-element.13) | copy-start | bytes 393220
  84.9 4.5 %copy-start.2 = (f32[1,128]{1,0:T(1,128)S(1)}, f32[1,128]{1,0:T(1,128)}, u32[]{:S(2)}) copy-start(f32[1,128]{1,0:T(1,128)} %get-tuple-element.8) | copy-start | bytes 1540

commit v3 on v2

--- a/solution.py
+++ b/solution.py
@@ -163,25 +163,34 @@
             self.copies[w].wait_recv()
 
     def round1(self):
-        for direction in range(3):
-            self.send(direction, 0, slice(None), 0)
+        self.send(0, 0, 0, 0)
+        self.send(1, 0, 1, 0)
+        self.send(0, 2, 1, 0)
+        self.send(1, 2, 0, 0)
+        self.send(2, 0, slice(None), 0)
 
     def round2(self):
         self.recv((0, 0))
         self.send(0, 1, 0, -1)
-        self.send(2, 1, slice(None), -1)
+        self.send(2, 1, 0, -1)
         self.recv((1, 0))
         self.send(1, 1, 1, 1)
-        self.send(2, 2, slice(None), 1)
+        self.send(2, 2, 1, 1)
 
     def round3(self):
+        self.recv((0, 2))
+        self.send(2, 3, 1, -1)
+        self.recv((1, 2))
+        self.send(2, 4, 0, 1)
+
+    def round4(self):
         self.recv((0, 1))
-        self.send(2, 3, 0, 2)
+        self.send(2, 5, 0, 2)
         self.recv((1, 1))
-        self.send(2, 4, 1, 2)
+        self.send(2, 6, 1, 2)
 
     def finish(self):
-        for slot in range(5):
+        for slot in range(7):
             self.recv((2, slot))
 
     def drain(self):
@@ -243,10 +252,10 @@
 def kernel(
     hidden_hbm, slot_ref, pos_ref, proj_hbm,
     pgrad_out, proj_out, loss_out,
-    hid, proj, pooled, pooled_in, pooled_t, uc, ur, ec, scores, weights, rowsum, colpart, zc, zr, zl, bias_c,
+    hid, proj, pooled, pooled_in, uc, ur, ec, scores, weights, rowsum, colpart, zc, zr, zl, bias_c,
     posterm, unit_s,
     g_full, g_out, g_sib, g_far, g_far_in, g_near, g_near_in, g_mid, g_mid_in,
-    p_full, p_out, p_sib, p_far, p_far_in, p_near, p_near_in, p_mid, p_mid_in,
+    p_full, p_out, p_sib, p_send, p_in,
     load_sem, uc_s, uc_r, ur_s, ur_r, ec_s, ec_r, g_s, g_r, p_s, p_r, a2a_s, a2a_r, zc_s, zc_r, zr_s, zr_r, zl_s, zl_r,
 ):
     dp, rep = lax.axis_index("dp"), lax.axis_index("rep")
@@ -340,6 +349,9 @@
     gr.round3()
     gc.second(0)
     gc.second(1)
+    gr.round4()
+    gc.cross(0)
+    gc.cross(1)
     gr.finish()
     rows = jnp.concatenate([ur[q // 2, q % 2] for q in range(4)], axis=1)
     live_r = ur[0, 0, :, 0:1].astype(F32) < 128.0
@@ -349,8 +361,6 @@
     bias_l = jnp.where(first[0:1] < 128.0, 0.0, NEG)
     nlive_r = jnp.sum(jnp.where(bias_l < -1.0, 0.0, 1.0), axis=1, keepdims=True)
     sum_r = pair_sums([(0, 0)], True)
-    gc.cross(0)
-    gc.cross(1)
     gc.last(0)
     gc.last(1)
     sum_r = sum_r + pair_sums([(-1, 0), (1, 0), (0, -1), (0, 1)], False)
@@ -377,14 +387,6 @@
         zcopies.append(rcopy(zr.at[rep], zr.at[rep], zr_s.at[j], zr_r.at[j], rep_peers[j]))
         zcopies[-1].start()
 
-    a2a = []
-    for j in range(15):
-        peer = dp_peers[j]
-        c = rcopy(pooled.at[peer[0]], pooled_in.at[at_c], a2a_s.at[j], a2a_r.at[j], peer)
-        c.start()
-        a2a.append(c)
-    pooled_in[at_c, :] = pooled[dp]
-
     id_r = lax.broadcasted_iota(jnp.int32, (ROWS, 1), 0) - rep * CAP
     id_r = jnp.where(jnp.logical_and(id_r >= 0, id_r < CAP), id_r, -1)
 
@@ -412,33 +414,41 @@
         total_r = total_r + zr[j]
     nlive = total_c[:, COLS : COLS + 1]
     log_c = jnp.where(bias_c[...] < -1.0, 0.0, jnp.log(total_c[:, :COLS]))
+    bias_c[...] = log_c * LOG2E
+    log_r = jnp.broadcast_to(jnp.log(total_r) * LOG2E, (128, ROWS)).T
+    log_r = jnp.where(live_r, log_r, 0.0)
+    rowsum[...] = log_r
+
+    def weight_tile(t, carry):
+        at = pl.ds(pl.multiple_of(t * 128, 128), 128)
+        s = scores[:, at]
+        w = jnp.exp2(s - rowsum[...]) + jnp.exp2(s - bias_c[:, at])
+        weights[:, at] = w.astype(BF16)
+        return carry
+
+    lax.fori_loop(0, 10, weight_tile, 0)
+
+    red = ReduceRep(g_full, g_out, g_sib, g_far, g_far_in, g_near, g_near_in, g_mid, g_mid_in, g_s, g_r, dp, x, k)
+    for q in ORDER:
+        red.put(q, jnp.dot(weights[...], uc[q // 2, q % 2], preferred_element_type=F32))
+    for q in ORDER:
+        red.step1(q)
+    a2a = []
+    for j in range(15):
+        peer = dp_peers[j]
+        c = rcopy(pooled.at[peer[0]], pooled_in.at[at_c], a2a_s.at[j], a2a_r.at[j], peer)
+        c.start()
+        a2a.append(c)
+    pooled_in[at_c, :] = pooled[dp]
+
+    for q in ORDER:
+        red.step2(q)
     loss_c = jnp.sum(log_c, axis=1, keepdims=True) - total_c[:, COLS + 1 : COLS + 2]
     zl[rep] = jnp.broadcast_to(loss_c, (1, 128))
     lcopies = []
     for j in range(7):
         lcopies.append(rcopy(zl.at[rep], zl.at[rep], zl_s.at[j], zl_r.at[j], rep_peers[j]))
         lcopies[-1].start()
-    bias_c[...] = log_c * LOG2E
-    log_r = jnp.broadcast_to(jnp.log(total_r) * LOG2E, (128, ROWS)).T
-    log_r = jnp.where(live_r, log_r, 0.0)
-    rowsum[...] = log_r
-
-    def weight_tile(t, carry):
-        at = pl.ds(pl.multiple_of(t * 128, 128), 128)
-        s = scores[:, at]
-        w = jnp.exp2(s - rowsum[...]) + jnp.exp2(s - bias_c[:, at])
-        weights[:, at] = w.astype(BF16)
-        return carry
-
-    lax.fori_loop(0, 10, weight_tile, 0)
-
-    red = ReduceRep(g_full, g_out, g_sib, g_far, g_far_in, g_near, g_near_in, g_mid, g_mid_in, g_s, g_r, dp, x, k)
-    for q in ORDER:
-        red.put(q, jnp.dot(weights[...], uc[q // 2, q % 2], preferred_element_type=F32))
-    for q in ORDER:
-        red.step1(q)
-    for q in ORDER:
-        red.step2(q)
     got = jnp.concatenate([red.result(q) for q in range(4)], axis=1)
     unit = unit_s[...]
     ugrad = (got - posterm[...]) * (MULT / nlive)
@@ -454,11 +464,18 @@
         part = lax.dot_general(egrad, proj[at, :], (((1,), (1,)), ((), ())), preferred_element_type=F32)
         pgrad_out[:, at] = (part / denom).astype(BF16)
 
+    def proj_part(blocks, begin=False):
+        left = jnp.concatenate([pooled_in[ge.at(*b), :] for b in blocks], axis=0).astype(F32).T.astype(BF16)
+        for q in range(4):
+            right = jnp.concatenate([ec[q // 2, q % 2, ge.at(*b), :] for b in blocks], axis=0)
+            part = jnp.dot(left, right, preferred_element_type=F32).reshape(4, 2, 32, 256)
+            p_full[q] = part if begin else p_full[q] + part
+
     ge.start(0)
     ge.start(1)
     for c in a2a:
         c.wait_recv()
-    pooled_t[...] = pooled_in[...].astype(F32).T.astype(BF16)
+    proj_part([(0, 0)], True)
     ge.first(0)
     ge.first(1)
     pgrad(0)
@@ -475,19 +492,35 @@
     ge.last(1)
     for j in range(4, 8):
         pgrad(j)
-    for slot in (9, 5, 6, 7):
+    proj_part([(-1, 0), (1, 0), (0, -1), (0, 1)])
+    for direction in range(4):
+        ge.recv((direction, 9))
+    proj_part([(-1, -1), (-1, 1), (1, -1), (1, 1), (2, 0), (0, 2)])
+    for slot in (5, 6):
         for direction in range(4):
             ge.recv((direction, slot))
-
-    red2 = ReduceRep(p_full, p_out, p_sib, p_far, p_far_in, p_near, p_near_in, p_mid, p_mid_in, p_s, p_r, dp, x, k)
-    for q in ORDER:
-        red2.put(q, jnp.dot(pooled_t[...], ec[q // 2, q % 2], preferred_element_type=F32))
-    for q in ORDER:
-        red2.step1(q)
-    for q in ORDER:
-        red2.step2(q)
+    proj_part([(-1, 2), (1, 2), (2, -1), (2, 1)])
+    for direction in range(4):
+        ge.recv((direction, 7))
+    proj_part([(2, 2)])
+
+    p_out[...] = p_full[:, :, 1 - k].astype(BF16)
+    pcopy = rcopy(p_out, p_sib, p_s.at[3], p_r.at[3], (dp, x * 2 + 1 - k))
+    pcopy.start()
+    pcopy.wait_recv()
+    pcopies = [pcopy]
+    for j in range(1, 4):
+        to = (x + j) % 4
+        p_send[j - 1] = (p_full[:, to, k] + p_sib[:, to].astype(F32)).astype(BF16)
+        c = rcopy(p_send.at[j - 1], p_in.at[j - 1], p_s.at[j - 1], p_r.at[j - 1], (dp, to * 2 + k))
+        c.start()
+        pcopies.append(c)
+    total = p_full[:, x, k] + p_sib[:, x].astype(F32)
+    for c in pcopies[1:]:
+        c.wait_recv()
+    total = total + p_in[0].astype(F32) + p_in[1].astype(F32) + p_in[2].astype(F32)
     for q in range(4):
-        proj_out[:, q * 256 : (q + 1) * 256] = red2.result(q)
+        proj_out[:, q * 256 : (q + 1) * 256] = total[q]
 
     for c in lcopies:
         c.wait_recv()
@@ -496,9 +529,9 @@
         loss = loss + zl[j]
     loss_out[...] = loss / nlive
 
-    for group in (gc, gr, red, ge, red2):
+    for group in (gc, gr, red, ge):
         group.drain()
-    for c in a2a + zcopies + lcopies:
+    for c in a2a + zcopies + lcopies + pcopies:
         c.wait_send()
 
 
@@ -510,6 +543,7 @@
 
 def local(hidden, step_slot, positive, proj):
     dma = pltpu.SemaphoreType.DMA
+    slots = step_slot.reshape(1, TOK)
     vm = pl.BlockSpec(memory_space=pltpu.VMEM)
     hbm = pl.BlockSpec(memory_space=pl.ANY)
     pooled_grad, proj_grad, loss = pl.pallas_call(
@@ -526,7 +560,6 @@
             pltpu.VMEM((D, F), BF16),
             pltpu.VMEM((16, CAP, 256), BF16),
             pltpu.VMEM((COLS, 256), BF16),
-            pltpu.VMEM((256, COLS), BF16),
             pltpu.VMEM((2, 2, COLS, 256), BF16),
             pltpu.VMEM((2, 2, ROWS, 256), BF16),
             pltpu.VMEM((2, 2, COLS, 256), BF16),
@@ -542,18 +575,24 @@
             pltpu.VMEM((CAP, F), F32),
         ]
         + reduce_scratch(CAP, BF16)
-        + reduce_scratch(32, BF16)
+        + [
+            pltpu.VMEM((4, 4, 2, 32, 256), F32),
+            pltpu.VMEM((4, 4, 32, 256), BF16),
+            pltpu.VMEM((4, 4, 32, 256), BF16),
+            pltpu.VMEM((3, 4, 32, 256), BF16),
+            pltpu.VMEM((3, 4, 32, 256), BF16),
+        ]
         + [
             dma((2, 4)),
-            dma((4, 10)), dma((4, 10)), dma((3, 5)), dma((3, 5)), dma((4, 10)), dma((4, 10)),
-            dma((4, 4)), dma((4, 4)), dma((4, 4)), dma((4, 4)),
+            dma((4, 10)), dma((4, 10)), dma((3, 7)), dma((3, 7)), dma((4, 10)), dma((4, 10)),
+            dma((4, 4)), dma((4, 4)), dma((4,)), dma((4,)),
             dma((15,)), dma((15,)), dma((15,)), dma((15,)), dma((7,)), dma((7,)), dma((7,)), dma((7,)),
         ],
         compiler_params=pltpu.CompilerParams(
             collective_id=0, has_side_effects=True, vmem_limit_bytes=60 * 1024 * 1024
         ),
         cost_estimate=pl.CostEstimate(flops=6_000_000_000, bytes_accessed=14_000_000, transcendentals=2_000_000),
-    )(hidden, step_slot.reshape(1, TOK), positive.reshape(1, CAP), proj)
+    )(hidden, slots, positive.reshape(1, CAP), proj)
     onehot = (step_slot[None, :] == lax.broadcasted_iota(jnp.int32, (CAP, TOK), 0)).astype(BF16)
     hidden_grad = lax.dot_general(onehot, pooled_grad, (((0,), (0,)), ((), ())), preferred_element_type=F32)
     return (hidden_grad.astype(BF16), proj_grad, loss[0, 0])

time: 90.7 us -> 87.2 us (0.961); the launches traced: 90.5 us -> 85.5 us
  Pallas kernels: 83 us -> 77.9 us
    pallas_call x1, Pallas kernels: 83 us -> 77.9 us  [local(): pl.pallas_call(kernel, out_shape=(jax.ShapeDtypeStruct((CAP, D), BF16), j...]
where the time goes in v3:
time: 87.2 us; the launch traced here: 85.5 us
  Pallas kernels  77.9 us (89%)
  matrix products  3.82 us (4%)
  local copies, waits for them, and re-layouts  1.91 us (2%)
  between operations  1.83 us (2%)
    pallas_call x1, Pallas kernels, local(): pl.pallas_call(kernel, out_shape=(jax.ShapeDtypeStruct((CAP, D), BF16), j...  77.9 us
    dot_general x1, matrix products, local(): lax.dot_general(onehot, pooled_grad, (((0,), (0,)), ((), ())), preferred_...  3.82 us

profile of v3, /device:TPU:0, one launch (start us, length us, event | category | flops | bytes accessed | tf_op | source)
XLA Modules:
  0.0 85.5 jit_solution(15259936474716465579)
XLA Ops:
  0.6 1.2 %broadcast_in_dim.3.slot_ref = s32[1,384]{1,0:T(1,128)} reshape(s32[384]{0:T(512)} %param.5) | data formatting | bytes 3072 | tf_op jit(solution)/shard_map/broadcast_in_dim | solution.py:596
  1.9 0.0 copy-start.1
  1.9 77.9 %shard_map.67 = (bf16[80,4096]{1,0:T(8,128)(2,1)}, f32[32,1024]{1,0:T(8,128)}, f32[1,128]{1,0:T(1,128)}) custom-call(bf16[384,4096]{1,0:T(8,128)(2,1)} %hidden_hbm.1, s32[1,384]{1,0:T(1,128)} %broadcast_in_dim.3.slot_ref, s32[1,80]{1,0:T(1,128)} %bitcast.4, bf16[4096,1024]{1,0:T(8,128)(2,1)} %proj_hbm.1), custom_call_target="tpu_custom_call" | custom-call | flops 6000000000 | bytes 14000000 | tf_op jit(solution)/shard_map/pallas_call | solution.py:549
  79.8 0.0 copy-start
  79.8 0.0 copy-start.2
  79.8 0.0 copy-done.1
  79.9 3.8 %convolution_convert_fusion = bf16[384,4096]{1,0:T(8,128)(2,1)} fusion(bf16[80,4096]{1,0:T(8,128)(2,1)} %get-tuple-element.6, s32[384]{0:T(512)S(1)} %copy-done.1), kind=kOutput, calls=%fused_computation | convolution fusion | flops 253261824 | bytes 3802624 | tf_op jit(solution)/shard_map/dot_general | solution.py:597
  83.7 0.0 copy-done
  83.7 0.7 copy.9
  84.3 0.0 copy-done.2
Async XLA Ops:
  1.9 78.0 %copy-start.1 = (s32[384]{0:T(512)S(1)}, s32[384]{0:T(512)}, u32[]{:S(2)}) copy-start(s32[384]{0:T(512)} %param.5) | copy-start | bytes 4612
  79.8 3.8 %copy-start = (f32[32,1024]{1,0:T(8,128)S(1)}, f32[32,1024]{1,0:T(8,128)}, u32[]{:S(2)}) copy-start(f32[32,1024]{1,0:T(8,128)} %get-tuple-element.13) | copy-start | bytes 393220
  79.8 4.5 %copy-start.2 = (f32[1,128]{1,0:T(1,128)S(1)}, f32[1,128]{1,0:T(1,128)}, u32[]{:S(2)}) copy-start(f32[1,128]{1,0:T(1,128)} %get-tuple-element.8) | copy-start | bytes 1540

commit v4 on v3

--- a/solution.py
+++ b/solution.py
@@ -251,11 +251,11 @@
 
 def kernel(
     hidden_hbm, slot_ref, pos_ref, proj_hbm,
-    pgrad_out, proj_out, loss_out,
+    pgrad_out, proj_out, part_out1, part_out2, part_out3, loss_out,
     hid, proj, pooled, pooled_in, uc, ur, ec, scores, weights, rowsum, colpart, zc, zr, zl, bias_c,
     posterm, unit_s,
     g_full, g_out, g_sib, g_far, g_far_in, g_near, g_near_in, g_mid, g_mid_in,
-    p_full, p_out, p_sib, p_send, p_in,
+    p_full, p_out, p_sib,
     load_sem, uc_s, uc_r, ur_s, ur_r, ec_s, ec_r, g_s, g_r, p_s, p_r, a2a_s, a2a_r, zc_s, zc_r, zr_s, zr_r, zl_s, zl_r,
 ):
     dp, rep = lax.axis_index("dp"), lax.axis_index("rep")
@@ -280,7 +280,7 @@
     for peer in near:
         pl.semaphore_signal(barrier, inc=1, device_id=peer, device_id_type=MESH)
 
-    member = slot_ref[...] == lax.broadcasted_iota(jnp.int32, (CAP, TOK), 0)
+    member = slot_ref[...].reshape(1, TOK) == lax.broadcasted_iota(jnp.int32, (CAP, TOK), 0)
     onehot = member.astype(F32)
     counts = jnp.sum(onehot, axis=1, keepdims=True)
     onehot = onehot.astype(BF16)
@@ -508,17 +508,13 @@
     pcopy = rcopy(p_out, p_sib, p_s.at[3], p_r.at[3], (dp, x * 2 + 1 - k))
     pcopy.start()
     pcopy.wait_recv()
-    pcopies = [pcopy]
+    part_outs = (part_out1, part_out2, part_out3)
     for j in range(1, 4):
         to = (x + j) % 4
-        p_send[j - 1] = (p_full[:, to, k] + p_sib[:, to].astype(F32)).astype(BF16)
-        c = rcopy(p_send.at[j - 1], p_in.at[j - 1], p_s.at[j - 1], p_r.at[j - 1], (dp, to * 2 + k))
-        c.start()
-        pcopies.append(c)
+        part = (p_full[:, to, k] + p_sib[:, to].astype(F32)).astype(BF16)
+        for q in range(4):
+            part_outs[j - 1][:, q * 256 : (q + 1) * 256] = part[q]
     total = p_full[:, x, k] + p_sib[:, x].astype(F32)
-    for c in pcopies[1:]:
-        c.wait_recv()
-    total = total + p_in[0].astype(F32) + p_in[1].astype(F32) + p_in[2].astype(F32)
     for q in range(4):
         proj_out[:, q * 256 : (q + 1) * 256] = total[q]
 
@@ -531,7 +527,7 @@
 
     for group in (gc, gr, red, ge):
         group.drain()
-    for c in a2a + zcopies + lcopies + pcopies:
+    for c in a2a + zcopies + lcopies + [pcopy]:
         c.wait_send()
 
 
@@ -543,18 +539,20 @@
 
 def local(hidden, step_slot, positive, proj):
     dma = pltpu.SemaphoreType.DMA
-    slots = step_slot.reshape(1, TOK)
     vm = pl.BlockSpec(memory_space=pltpu.VMEM)
     hbm = pl.BlockSpec(memory_space=pl.ANY)
-    pooled_grad, proj_grad, loss = pl.pallas_call(
+    pooled_grad, proj_grad, part1, part2, part3, loss = pl.pallas_call(
         kernel,
         out_shape=(
             jax.ShapeDtypeStruct((CAP, D), BF16),
             jax.ShapeDtypeStruct((32, F), F32),
+            jax.ShapeDtypeStruct((32, F), BF16),
+            jax.ShapeDtypeStruct((32, F), BF16),
+            jax.ShapeDtypeStruct((32, F), BF16),
             jax.ShapeDtypeStruct((1, 128), F32),
         ),
         in_specs=[hbm, vm, vm, hbm],
-        out_specs=(vm, vm, vm),
+        out_specs=(vm,) * 6,
         scratch_shapes=[
             pltpu.VMEM((4, TOK, 1024), BF16),
             pltpu.VMEM((D, F), BF16),
@@ -579,8 +577,6 @@
             pltpu.VMEM((4, 4, 2, 32, 256), F32),
             pltpu.VMEM((4, 4, 32, 256), BF16),
             pltpu.VMEM((4, 4, 32, 256), BF16),
-            pltpu.VMEM((3, 4, 32, 256), BF16),
-            pltpu.VMEM((3, 4, 32, 256), BF16),
         ]
         + [
             dma((2, 4)),
@@ -592,7 +588,10 @@
             collective_id=0, has_side_effects=True, vmem_limit_bytes=60 * 1024 * 1024
         ),
         cost_estimate=pl.CostEstimate(flops=6_000_000_000, bytes_accessed=14_000_000, transcendentals=2_000_000),
-    )(hidden, slots, positive.reshape(1, CAP), proj)
+    )(hidden, step_slot, positive.reshape(1, CAP), proj)
+    for j, part in ((1, part1), (3, part3), (2, part2)):
+        ring = [(d, (d // 2 + j) % 4 * 2 + d % 2) for d in range(8)]
+        proj_grad = proj_grad + lax.ppermute(part, "rep", ring).astype(F32)
     onehot = (step_slot[None, :] == lax.broadcasted_iota(jnp.int32, (CAP, TOK), 0)).astype(BF16)
     hidden_grad = lax.dot_general(onehot, pooled_grad, (((0,), (0,)), ((), ())), preferred_element_type=F32)
     return (hidden_grad.astype(BF16), proj_grad, loss[0, 0])

time: 87.2 us -> 84.9 us (0.974); the launches traced: 85.5 us -> 84.7 us
  Pallas kernels: 77.9 us -> 72.9 us
  starting transfers between devices: 0 us -> 4.45 us
  local copies, waits for them, and re-layouts: 1.91 us -> 0.01 us
  waiting for transfers between devices: 0 us -> 1.05 us
    pallas_call x1, Pallas kernels: 77.9 us -> 72.9 us  [local(): pl.pallas_call(kernel, out_shape=(jax.ShapeDtypeStruct((CAP, D), BF16), j...]
    ppermute x0 -> x3, starting transfers between devices: none -> 4.45 us  [local(): proj_grad = proj_grad + lax.ppermute(part, 'rep', ring).astype(F32)]
    broadcast_in_dim x1 -> x0, local copies, waits for them, and re-layouts: 1.25 us -> none  [local(): step_slot[None, :] == lax.broadcasted_iota(jnp.int32, (CAP, TOK), 0)]
    ppermute x0 -> x3, waiting for transfers between devices: none -> 1.05 us  [local(): proj_grad = proj_grad + lax.ppermute(part, 'rep', ring).astype(F32)]
  transfers between devices with their start and end apart: 0 -> 3, of which waited for: 0 -> 1; matrix products, arithmetic and copies ran while one was open for 0% -> 4% of each run, Pallas kernels for 0% -> 0%
where the time goes in v4:
time: 84.9 us; the launch traced here: 84.7 us
  Pallas kernels  72.9 us (86%)
  starting transfers between devices  4.45 us (5%)
  matrix products  3.78 us (4%)
  between operations  1.83 us (2%)
  waiting for transfers between devices  1.05 us (1%)
    pallas_call x1, Pallas kernels, local(): pl.pallas_call(kernel, out_shape=(jax.ShapeDtypeStruct((CAP, D), BF16), j...  72.9 us
    ppermute x3, starting transfers between devices, local(): proj_grad = proj_grad + lax.ppermute(part, 'rep', ring).astype(F32)  4.45 us
    dot_general x1, matrix products, local(): lax.dot_general(onehot, pooled_grad, (((0,), (0,)), ((), ())), preferred_...  3.78 us
  transfers between devices with their start and end apart: 3, of which 1 were waited for; matrix products, arithmetic and copies ran while one was open for 4% of the time, Pallas kernels for 0%

profile of v4, /device:TPU:0, one launch (start us, length us, event | category | flops | bytes accessed | tf_op | source)
XLA Modules:
  0.0 84.7 jit_solution(2565735698632407684)
XLA Ops:
  0.6 0.0 copy-start.1
  0.6 72.9 %shard_map.67 = (bf16[80,4096]{1,0:T(8,128)(2,1)}, f32[32,1024]{1,0:T(8,128)}, bf16[32,1024]{1,0:T(8,128)(2,1)}, bf16[32,1024]{1,0:T(8,128)(2,1)}, bf16[32,1024]{1,0:T(8,128)(2,1)}, /*index=5*/f32[1,128]{1,0:T(1,128)}) custom-call(bf16[384,4096]{1,0:T(8,128)(2,1)} %hidden_hbm.1, s32[384]{0:T(512)} %slot_ref.1, s32[1,80]{1,0:T(1,128)} %bitcast.4, ...), custom_call_target="tpu_custom_call" | custom-call | flops 6000000000 | bytes 14000000 | tf_op jit(solution)/shard_map/pallas_call | solution.py:544
  73.6 0.0 copy-start
  73.6 0.0 copy-start.2
  73.6 0.9 %collective-permute-start = (bf16[32,1024]{1,0:T(8,128)(2,1)}, bf16[32,1024]{1,0:T(8,128)(2,1)S(1)}, u32[]{:S(2)}, u32[]{:S(2)}) collective-permute-start(bf16[32,1024]{1,0:T(8,128)(2,1)} %get-tuple-element.11), channel_id=1, source_target_pairs={{0,2},{1,3},{2,4},{3,5},{4,6},{5,7},{6,0},{7,1},{8,10},{9,11},{10,... | collective-permute-start | bytes 196616 | tf_op jit(solution)/shard_map/ppermute | solution.py:594
  74.4 2.4 %collective-permute-start.1 = (bf16[32,1024]{1,0:T(8,128)(2,1)}, bf16[32,1024]{1,0:T(8,128)(2,1)S(1)}, u32[]{:S(2)}, u32[]{:S(2)}) collective-permute-start(bf16[32,1024]{1,0:T(8,128)(2,1)} %get-tuple-element.12), channel_id=1, source_target_pairs={{0,6},{1,7},{2,0},{3,1},{4,2},{5,3},{6,4},{7,5},{8,14},{9,15},{10,... | collective-permute-start | bytes 196616 | tf_op jit(solution)/shard_map/ppermute | solution.py:594
  76.9 1.1 %collective-permute-start.2 = (bf16[32,1024]{1,0:T(8,128)(2,1)}, bf16[32,1024]{1,0:T(8,128)(2,1)S(1)}, u32[]{:S(2)}, u32[]{:S(2)}) collective-permute-start(bf16[32,1024]{1,0:T(8,128)(2,1)} %get-tuple-element.13), channel_id=1, source_target_pairs={{0,4},{1,5},{2,6},{3,7},{4,0},{5,1},{6,2},{7,3},{8,12},{9,13},{10,... | collective-permute-start | bytes 196616 | tf_op jit(solution)/shard_map/ppermute | solution.py:594
  78.0 0.0 copy-done.1
  78.0 3.8 %convolution_convert_fusion = bf16[384,4096]{1,0:T(8,128)(2,1)} fusion(bf16[80,4096]{1,0:T(8,128)(2,1)} %get-tuple-element.9, s32[384]{0:T(512)S(1)} %copy-done.1), kind=kOutput, calls=%fused_computation | convolution fusion | flops 253261824 | bytes 3802624 | tf_op jit(solution)/shard_map/dot_general | solution.py:596
  81.8 0.0 collective-permute-done
  81.8 0.0 collective-permute-done.1
  81.8 1.0 %collective-permute-done.2 = bf16[32,1024]{1,0:T(8,128)(2,1)S(1)} collective-permute-done((bf16[32,1024]{1,0:T(8,128)(2,1)}, bf16[32,1024]{1,0:T(8,128)(2,1)S(1)}, u32[]{:S(2)}, u32[]{:S(2)}) %collective-permute-start.2) | collective-permute-done | bytes 65568 | tf_op jit(solution)/shard_map/ppermute | solution.py:594
  82.9 0.0 copy-done
  82.9 0.7 convert_add_fusion
  83.6 0.0 copy-done.2
Async XLA Ops:
  0.6 77.4 %copy-start.1 = (s32[384]{0:T(512)S(1)}, s32[384]{0:T(512)}, u32[]{:S(2)}) copy-start(s32[384]{0:T(512)} %slot_ref.1) | copy-start | bytes 4612
  73.6 9.3 %copy-start = (f32[32,1024]{1,0:T(8,128)S(1)}, f32[32,1024]{1,0:T(8,128)}, u32[]{:S(2)}) copy-start(f32[32,1024]{1,0:T(8,128)} %get-tuple-element.10) | copy-start | bytes 393220
  73.6 10.0 %copy-start.2 = (f32[1,128]{1,0:T(1,128)S(1)}, f32[1,128]{1,0:T(1,128)}, u32[]{:S(2)}) copy-start(f32[1,128]{1,0:T(1,128)} %get-tuple-element.14) | copy-start | bytes 1540
  73.6 8.2 %collective-permute-start = (bf16[32,1024]{1,0:T(8,128)(2,1)}, bf16[32,1024]{1,0:T(8,128)(2,1)S(1)}, u32[]{:S(2)}, u32[]{:S(2)}) collective-permute-start(bf16[32,1024]{1,0:T(8,128)(2,1)} %get-tuple-element.11), channel_id=1, source_target_pairs={{0,2},{1,3},{2,4},{3,5},{4,6},{5,7},{6,0},{7,1},{8,10},{9,11},{10,... | collective-permute-start | bytes 196616 | tf_op jit(solution)/shard_map/ppermute | solution.py:594
  74.4 7.4 %collective-permute-start.1 = (bf16[32,1024]{1,0:T(8,128)(2,1)}, bf16[32,1024]{1,0:T(8,128)(2,1)S(1)}, u32[]{:S(2)}, u32[]{:S(2)}) collective-permute-start(bf16[32,1024]{1,0:T(8,128)(2,1)} %get-tuple-element.12), channel_id=1, source_target_pairs={{0,6},{1,7},{2,0},{3,1},{4,2},{5,3},{6,4},{7,5},{8,14},{9,15},{10,... | collective-permute-start | bytes 196616 | tf_op jit(solution)/shard_map/ppermute | solution.py:594
  76.9 6.0 %collective-permute-start.2 = (bf16[32,1024]{1,0:T(8,128)(2,1)}, bf16[32,1024]{1,0:T(8,128)(2,1)S(1)}, u32[]{:S(2)}, u32[]{:S(2)}) collective-permute-start(bf16[32,1024]{1,0:T(8,128)(2,1)} %get-tuple-element.13), channel_id=1, source_target_pairs={{0,4},{1,5},{2,6},{3,7},{4,0},{5,1},{6,2},{7,3},{8,12},{9,13},{10,... | collective-permute-start | bytes 196616 | tf_op jit(solution)/shard_map/ppermute | solution.py:594

commit v5 on v4

--- a/solution.py
+++ b/solution.py
@@ -28,6 +28,10 @@
     return pltpu.make_async_remote_copy(
         src_ref=src, dst_ref=dst, send_sem=send_sem, recv_sem=recv_sem, device_id=device, device_id_type=MESH
     )
+
+
+FLIGHT = 8
+GRP = 2
 
 
 class GatherDp:
@@ -263,16 +267,15 @@
     dp_peers = [((dp + j) % 16, rep) for j in range(1, 16)]
     rep_peers = [(dp, (rep + j) % 8) for j in range(1, 8)]
 
-    loads = []
-    for j in range(4):
-        loads.append(
-            (
-                pltpu.make_async_copy(hidden_hbm.at[:, pl.ds(j * 1024, 1024)], hid.at[j], load_sem.at[0, j]),
-                pltpu.make_async_copy(proj_hbm.at[pl.ds(j * 1024, 1024)], proj.at[pl.ds(j * 1024, 1024)], load_sem.at[1, j]),
-            )
-        )
-        loads[-1][0].start()
-        loads[-1][1].start()
+    hloads = [
+        pltpu.make_async_copy(hidden_hbm.at[:, pl.ds(j * 1024, 1024)], hid.at[j], load_sem.at[j]) for j in range(4)
+    ]
+    ploads = [
+        pltpu.make_async_copy(proj_hbm.at[pl.ds(j * 512, 512)], proj.at[pl.ds(j * 512, 512)], load_sem.at[4 + j])
+        for j in range(8)
+    ]
+    for c in hloads + ploads[:FLIGHT]:
+        c.start()
 
     barrier = pltpu.get_barrier_semaphore()
     near = [((z + 1) % 4 * 4 + y, rep), ((z + 3) % 4 * 4 + y, rep), (z * 4 + (y + 1) % 4, rep), (z * 4 + (y + 3) % 4, rep)]
@@ -287,13 +290,18 @@
     denom = jnp.maximum(counts, 1.0)
     live = counts > 0.0
     embed = jnp.zeros((CAP, F), F32)
+    chunks = []
     for j in range(4):
-        loads[j][0].wait()
+        hloads[j].wait()
         chunk = (jnp.dot(onehot, hid[j], preferred_element_type=F32) / denom).astype(BF16)
         for i in range(4):
             pooled[j * 4 + i] = chunk[:, i * 256 : (i + 1) * 256]
-        loads[j][1].wait()
-        embed = embed + jnp.dot(chunk, proj[pl.ds(j * 1024, 1024), :], preferred_element_type=F32)
+        chunks += [chunk[:, :512], chunk[:, 512:]]
+    for j in range(8):
+        ploads[j].wait()
+        if j + FLIGHT < 8:
+            ploads[j + FLIGHT].start()
+        embed = embed + jnp.dot(chunks[j], proj[pl.ds(j * 512, 512), :], preferred_element_type=F32)
     rscale = lax.rsqrt(jnp.mean(embed * embed, axis=1, keepdims=True) + 1e-06)
     unit = embed * rscale
     unit_s[...] = unit
@@ -429,8 +437,11 @@
     lax.fori_loop(0, 10, weight_tile, 0)
 
     red = ReduceRep(g_full, g_out, g_sib, g_far, g_far_in, g_near, g_near_in, g_mid, g_mid_in, g_s, g_r, dp, x, k)
-    for q in ORDER:
-        red.put(q, jnp.dot(weights[...], uc[q // 2, q % 2], preferred_element_type=F32))
+    for first_q in range(0, 4, GRP):
+        right = jnp.concatenate([uc[q // 2, q % 2] for q in range(first_q, first_q + GRP)], axis=1)
+        both = jnp.dot(weights[...], right, preferred_element_type=F32)
+        for q in range(GRP):
+            red.put(first_q + q, both[:, q * 256 : (q + 1) * 256])
     for q in ORDER:
         red.step1(q)
     a2a = []
@@ -579,7 +590,7 @@
             pltpu.VMEM((4, 4, 32, 256), BF16),
         ]
         + [
-            dma((2, 4)),
+            dma((12,)),
             dma((4, 10)), dma((4, 10)), dma((3, 7)), dma((3, 7)), dma((4, 10)), dma((4, 10)),
             dma((4, 4)), dma((4, 4)), dma((4,)), dma((4,)),
             dma((15,)), dma((15,)), dma((15,)), dma((15,)), dma((7,)), dma((7,)), dma((7,)), dma((7,)),

time: 84.9 us -> 83.1 us (0.979)
  Pallas kernels: 72.9 us -> 71.1 us
    pallas_call x1, Pallas kernels: 72.9 us -> 71.1 us  [local(): pl.pallas_call(kernel, out_shape=(jax.ShapeDtypeStruct((CAP, D), BF16), j...]
  transfers between devices with their start and end apart: 3 -> 3, of which waited for: 1 -> 1; matrix products, arithmetic and copies ran while one was open for 4% -> 5% of each run, Pallas kernels for 0% -> 0%
where the time goes in v5:
time: 83.1 us; the launch traced here: 82.9 us
  Pallas kernels  71.1 us (86%)
  starting transfers between devices  4.33 us (5%)
  matrix products  3.78 us (5%)
  between operations  1.83 us (2%)
  waiting for transfers between devices  1.17 us (1%)
    pallas_call x1, Pallas kernels, local(): pl.pallas_call(kernel, out_shape=(jax.ShapeDtypeStruct((CAP, D), BF16), j...  71.1 us
    ppermute x3, starting transfers between devices, local(): proj_grad = proj_grad + lax.ppermute(part, 'rep', ring).astype(F32)  4.33 us
    dot_general x1, matrix products, local(): lax.dot_general(onehot, pooled_grad, (((0,), (0,)), ((), ())), preferred_...  3.78 us
  transfers between devices with their start and end apart: 3, of which 1 were waited for; matrix products, arithmetic and copies ran while one was open for 5% of the time, Pallas kernels for 0%

profile of v5, /device:TPU:0, one launch (start us, length us, event | category | flops | bytes accessed | tf_op | source)
XLA Modules:
  0.0 82.9 jit_solution(1210489864949495987)
XLA Ops:
  0.6 0.0 copy-start.1
  0.6 71.1 %shard_map.67 = (bf16[80,4096]{1,0:T(8,128)(2,1)}, f32[32,1024]{1,0:T(8,128)}, bf16[32,1024]{1,0:T(8,128)(2,1)}, bf16[32,1024]{1,0:T(8,128)(2,1)}, bf16[32,1024]{1,0:T(8,128)(2,1)}, /*index=5*/f32[1,128]{1,0:T(1,128)}) custom-call(bf16[384,4096]{1,0:T(8,128)(2,1)} %hidden_hbm.1, s32[384]{0:T(512)} %slot_ref.1, s32[1,80]{1,0:T(1,128)} %bitcast.4, ...), custom_call_target="tpu_custom_call" | custom-call | flops 6000000000 | bytes 14000000 | tf_op jit(solution)/shard_map/pallas_call | solution.py:555
  71.7 0.0 copy-start
  71.7 0.0 copy-start.2
  71.8 0.7 collective-permute-start
  72.5 2.6 %collective-permute-start.1 = (bf16[32,1024]{1,0:T(8,128)(2,1)}, bf16[32,1024]{1,0:T(8,128)(2,1)S(1)}, u32[]{:S(2)}, u32[]{:S(2)}) collective-permute-start(bf16[32,1024]{1,0:T(8,128)(2,1)} %get-tuple-element.12), channel_id=1, source_target_pairs={{0,6},{1,7},{2,0},{3,1},{4,2},{5,3},{6,4},{7,5},{8,14},{9,15},{10,... | collective-permute-start | bytes 196616 | tf_op jit(solution)/shard_map/ppermute | solution.py:605
  75.1 1.0 %collective-permute-start.2 = (bf16[32,1024]{1,0:T(8,128)(2,1)}, bf16[32,1024]{1,0:T(8,128)(2,1)S(1)}, u32[]{:S(2)}, u32[]{:S(2)}) collective-permute-start(bf16[32,1024]{1,0:T(8,128)(2,1)} %get-tuple-element.13), channel_id=1, source_target_pairs={{0,4},{1,5},{2,6},{3,7},{4,0},{5,1},{6,2},{7,3},{8,12},{9,13},{10,... | collective-permute-start | bytes 196616 | tf_op jit(solution)/shard_map/ppermute | solution.py:605
  76.1 0.0 copy-done.1
  76.1 3.8 %convolution_convert_fusion = bf16[384,4096]{1,0:T(8,128)(2,1)} fusion(bf16[80,4096]{1,0:T(8,128)(2,1)} %get-tuple-element.9, s32[384]{0:T(512)S(1)} %copy-done.1), kind=kOutput, calls=%fused_computation | convolution fusion | flops 253261824 | bytes 3802624 | tf_op jit(solution)/shard_map/dot_general | solution.py:607
  79.9 0.0 collective-permute-done
  79.9 0.0 collective-permute-done.1
  79.9 1.2 %collective-permute-done.2 = bf16[32,1024]{1,0:T(8,128)(2,1)S(1)} collective-permute-done((bf16[32,1024]{1,0:T(8,128)(2,1)}, bf16[32,1024]{1,0:T(8,128)(2,1)S(1)}, u32[]{:S(2)}, u32[]{:S(2)}) %collective-permute-start.2) | collective-permute-done | bytes 65568 | tf_op jit(solution)/shard_map/ppermute | solution.py:605
  81.0 0.0 copy-done
  81.0 0.7 convert_add_fusion
  81.7 0.0 copy-done.2
Async XLA Ops:
  0.6 75.5 %copy-start.1 = (s32[384]{0:T(512)S(1)}, s32[384]{0:T(512)}, u32[]{:S(2)}) copy-start(s32[384]{0:T(512)} %slot_ref.1) | copy-start | bytes 4612
  71.7 9.3 %copy-start = (f32[32,1024]{1,0:T(8,128)S(1)}, f32[32,1024]{1,0:T(8,128)}, u32[]{:S(2)}) copy-start(f32[32,1024]{1,0:T(8,128)} %get-tuple-element.10) | copy-start | bytes 393220
  71.7 10.0 %copy-start.2 = (f32[1,128]{1,0:T(1,128)S(1)}, f32[1,128]{1,0:T(1,128)}, u32[]{:S(2)}) copy-start(f32[1,128]{1,0:T(1,128)} %get-tuple-element.14) | copy-start | bytes 1540
  71.8 8.1 %collective-permute-start = (bf16[32,1024]{1,0:T(8,128)(2,1)}, bf16[32,1024]{1,0:T(8,128)(2,1)S(1)}, u32[]{:S(2)}, u32[]{:S(2)}) collective-permute-start(bf16[32,1024]{1,0:T(8,128)(2,1)} %get-tuple-element.11), channel_id=1, source_target_pairs={{0,2},{1,3},{2,4},{3,5},{4,6},{5,7},{6,0},{7,1},{8,10},{9,11},{10,... | collective-permute-start | bytes 196616 | tf_op jit(solution)/shard_map/ppermute | solution.py:605
  72.5 7.4 %collective-permute-start.1 = (bf16[32,1024]{1,0:T(8,128)(2,1)}, bf16[32,1024]{1,0:T(8,128)(2,1)S(1)}, u32[]{:S(2)}, u32[]{:S(2)}) collective-permute-start(bf16[32,1024]{1,0:T(8,128)(2,1)} %get-tuple-element.12), channel_id=1, source_target_pairs={{0,6},{1,7},{2,0},{3,1},{4,2},{5,3},{6,4},{7,5},{8,14},{9,15},{10,... | collective-permute-start | bytes 196616 | tf_op jit(solution)/shard_map/ppermute | solution.py:605
  75.1 6.0 %collective-permute-start.2 = (bf16[32,1024]{1,0:T(8,128)(2,1)}, bf16[32,1024]{1,0:T(8,128)(2,1)S(1)}, u32[]{:S(2)}, u32[]{:S(2)}) collective-permute-start(bf16[32,1024]{1,0:T(8,128)(2,1)} %get-tuple-element.13), channel_id=1, source_target_pairs={{0,4},{1,5},{2,6},{3,7},{4,0},{5,1},{6,2},{7,3},{8,12},{9,13},{10,... | collective-permute-start | bytes 196616 | tf_op jit(solution)/shard_map/ppermute | solution.py:605
